TPU v7x, 256 devices: a whole 4x4x8 slice. The times are simulated.
256 devices in a mesh: sub: 64 (over x, z, core), grp: 4 (over y).
Axes of the slice: x: 4, y: 4, z: 8, core: 2. Of those that a mesh axis runs over, the one named last changes fastest.
Arguments:
- multipliers: float32 [64, 4, 64, 1200], P('sub', 'grp'), as said below
- residual: float32 [64, 4, 64, 1200], P('sub', 'grp'), as said below
- direction: float32 [64, 4, 64, 1200], P('sub', 'grp'), as said below
- dual_operator: float32 [64, 4, 1200, 1200], P('sub', 'grp'), as said below
- rigid_trace: float32 [64, 4, 6, 1200], P('sub', 'grp'), may hold values from -0.375 to 0.375
- coarse_inverse: float32 [1536, 1536], P(('sub', 'grp'))
- face_sizes: int32 [64, 4, 4], P('sub', 'grp'), may hold values from 0 to 300, as said below
- slot_order: int32 [64, 4, 1200], P('sub', 'grp'), may hold values from 0 to 1199, each once within a row
Outputs:
- multipliers_next: float32 [64, 4, 64, 1200], P('sub', 'grp')
- residual_next: float32 [64, 4, 64, 1200], P('sub', 'grp')
- direction_next: float32 [64, 4, 64, 1200], P('sub', 'grp')
Inputs may be any that keep to these rules, and one draw needn't show every extreme that they name: `face_sizes`: face 0 of every subdomain with s = 0, face 1 with s = 63, face 2 with g = 0 and face 3 with g = 3 have size 0; the two faces that two subdomains share have equal sizes; the size 300 occurs in every draw. `multipliers`: where two subdomains share a face, their copies agree place by place: face 1 of (s, g) equals face 0 of (s + 1, g), face 3 of (s, g) equals face 2 of (s, g + 1). `residual`: copies on shared faces agree as for multipliers. `direction`: copies on shared faces agree as for multipliers. `dual_operator`: each block has a positive definite symmetric part.
All inputs are finite; a program needn't handle non-finite values.
Results may differ from a plain program's by a relative error of at most 0.000062.
Values sent between devices are 32-bit elements; how exact they have to be, the bound alone decides.
A program may use at most 64 MiB of HBM per device.

v0:
```python
import jax
import jax.numpy as jnp
from jax import lax
from jax.sharding import PartitionSpec as P


def with_halo(block, sides, width):
    for axis, dim in sides:
        count = lax.axis_size(axis)
        forward = [(i, i + 1) for i in range(count - 1)]
        backward = [(target, source) for source, target in forward]
        low = lax.ppermute(
            lax.slice_in_dim(block, block.shape[dim] - width, None, axis=dim), axis, forward
        )
        high = lax.ppermute(lax.slice_in_dim(block, 0, width, axis=dim), axis, backward)
        block = jnp.concatenate([low, block, high], axis=dim)
    return block


def assemble(field, face_width):
    cases = field.shape[0]
    faces = field.reshape(cases, 4, face_width)
    along_sub = jnp.stack([faces[:, 0], faces[:, 1]])
    got_sub = with_halo(along_sub, (("sub", 0),), 1)
    along_grp = jnp.stack([faces[:, 2], faces[:, 3]])
    got_grp = with_halo(along_grp, (("grp", 0),), 1)
    extra = jnp.stack([got_sub[0], got_sub[3], got_grp[0], got_grp[3]], axis=1)
    return field + extra.reshape(field.shape)


def on_device(
    multipliers,
    residual,
    direction,
    dual_operator,
    rigid_trace,
    coarse_inverse,
    face_sizes,
    slot_order,
):
    cases = multipliers.shape[2]
    width = multipliers.shape[3]
    face_width = width // 4
    high = lax.Precision.HIGHEST
    position = jnp.arange(width, dtype=jnp.int32)
    face_of = position // face_width
    pick = face_of[None, :] == jnp.arange(4, dtype=jnp.int32)[:, None]
    limit = jnp.sum(jnp.where(pick, face_sizes[0, 0][:, None], 0), axis=0)
    active = (position % face_width < limit).astype(jnp.float32)[None, :]
    face_sign = jnp.where(face_of % 2 == 0, -1.0, 1.0).astype(jnp.float32)
    order = slot_order[0, 0]
    inverse = jnp.argsort(order)
    slot_sign = face_sign[order][None, :]

    def to_slots(field):
        return field[:, order] * slot_sign

    def to_faces(values):
        return (values * slot_sign)[:, inverse] * active

    lam = multipliers[0, 0] * active
    res = residual[0, 0] * active
    dirn = direction[0, 0] * active
    dual = dual_operator[0, 0]
    trace = rigid_trace[0, 0]
    modes = trace.shape[0]
    applied = lax.dot_general(to_slots(dirn), dual, (((1,), (1,)), ((), ())), precision=high)
    own_faces = to_faces(applied)
    rr_local = 0.5 * jnp.sum(res * res, axis=1)
    image = assemble(own_faces, face_width)
    curv_local = 0.5 * jnp.sum(dirn * image, axis=1)
    coarse_local = lax.dot_general(trace, to_slots(image), (((1,), (1,)), ((), ())), precision=high)
    total = coarse_inverse.shape[1]
    dense = jnp.zeros((total, cases), jnp.float32)
    offset = lax.axis_index(("sub", "grp")) * modes
    dense = lax.dynamic_update_slice(dense, coarse_local, (offset, jnp.int32(0)))
    every, rr, curvature = lax.psum((dense, rr_local, curv_local), ("sub", "grp"))
    amplitude = jnp.dot(coarse_inverse, every, precision=high)
    back = lax.dot_general(amplitude, trace, (((0,), (0,)), ((), ())), precision=high)
    projected = image - assemble(to_faces(back), face_width)
    step = (rr / curvature)[:, None]
    lam_next = lam + step * dirn
    res_next = res - step * projected
    rr_next = lax.psum(0.5 * jnp.sum(res_next * res_next, axis=1), ("sub", "grp"))
    dir_next = res_next + (rr_next / rr)[:, None] * dirn
    return (lam_next[None, None], res_next[None, None], dir_next[None, None])


def solution(mesh):
    return jax.shard_map(
        on_device,
        mesh=mesh,
        in_specs=(
            P("sub", "grp", None, None),
            P("sub", "grp", None, None),
            P("sub", "grp", None, None),
            P("sub", "grp", None, None),
            P("sub", "grp", None, None),
            P(("sub", "grp"), None),
            P("sub", "grp", None),
            P("sub", "grp", None),
        ),
        out_specs=(
            P("sub", "grp", None, None),
            P("sub", "grp", None, None),
            P("sub", "grp", None, None),
        ),
        check_vma=False,
    )
```

profile of v0, /device:TPU:1, one launch (start us, length us, event | category | flops | bytes accessed | tf_op | source)
XLA Modules:
  0.0 491.9 jit_solution(16020288402623644236)
XLA Ops:
  7.2 0.0 copy-start
  7.2 0.0 all-reduce.3.cloned.1.call-start
  7.3 0.7 select_reduce_fusion
  8.0 0.1 reduce_sum.40
  8.1 0.7 fusion.33
  8.8 0.7 reduce.1
  9.6 5.1 %sort.17 = (s32[1200]{0:T(1024)}, s32[1200]{0:T(1024)S(1)}) sort(s32[1200]{0:T(1024)S(1)} %reduce.1, s32[1200]{0:T(1024)S(1)} %iota.39), dimensions={0}, to_apply=%region_3.4 | sort | flops 13200 | bytes 19200 | tf_op jit(solution)/shard_map/jit(argsort)/sort | solution.py:52
  14.7 1.0 bitcast_multiply_fusion.2
  15.7 0.2 copy.53
  15.9 6.8 %gather_fusion.1 = f32[1200]{0:T(1024)S(1)} fusion(f32[1200]{0:T(1024)S(1)} %fusion.26, s32[2048]{0:T(1024)S(1)} %pad_clamp_fusion.1), kind=kCustom, calls=%fused_computation.1 | custom fusion | bytes 14400 | tf_op jit(solution)/shard_map/gather | solution.py:53
  22.7 2.5 gather_fusion
  25.2 0.0 copy-start.2
  25.2 0.0 copy-start.3
  25.2 8.7 %fusion.2 = f32[64,1200]{1,0:T(8,128)S(1)} fusion(f32[1,1,1200,1200]{3,2,1,0:T(8,128)} %param.11, f32[1200,64]{1,0:T(8,128)S(1)} %gather_fusion, f32[1200]{0:T(1024)S(1)} %gather_fusion.1), kind=kOutput, calls=%fused_computation.7 | convolution fusion | flops 1106073600 | bytes 6379200 | tf_op jit(solution)/shard_map/dot_general | solution.py:67
  33.9 0.2 copy.54
  34.1 0.0 copy-start.5
  34.1 2.5 gather_fusion.2
  36.6 0.2 copy.55
  36.8 0.3 gather.26
  37.2 0.3 slice_bitcast_fusion.7
  37.5 4.9 %collective-permute-start = (f32[1,64,300]{2,0,1:T(1,128)S(1)}, f32[1,64,300]{2,0,1:T(1,128)S(1)}, u32[]{:S(2)}, u32[]{:S(2)}) collective-permute-start(f32[1,64,300]{2,0,1:T(1,128)S(1)} %get-tuple-element.24), channel_id=1, source_target_pairs={{0,4},{4,8},{8,12},{12,16},{16,20},{20,24},{24,28},{28,32},{32,36}... | collective-permute-start | bytes 230408 | tf_op jit(solution)/shard_map/ppermute | solution.py:12
  42.4 1.3 collective-permute-start.3
  43.7 4.0 collective-permute-start.2
  47.7 2.2 collective-permute-start.1
  50.0 0.0 collective-permute-done
  50.0 0.0 collective-permute-done.3
  50.0 0.0 collective-permute-done.2
  50.0 3.6 collective-permute-done.1
  53.7 0.4 pad_maximum_fusion
  54.0 0.2 reshape.246
  54.3 0.2 multiply_reduce_fusion.1
  54.5 0.2 copy.56
  54.7 2.5 gather_fusion.3
  57.2 0.0 copy-done.5
  57.2 0.5 convolution_bitcast_fusion
  57.8 0.1 broadcast_in_dim.47
  57.8 0.1 dynamic_update_slice.3
  58.0 0.9 copy-done.1
  58.9 0.0 all-reduce.3.cloned.1.call-update
  58.9 0.0 copy-start.4
  58.9 254.9 %all-reduce.3.cloned.1.call-done = f32[1536,64]{1,0:T(8,128)} async-done(((f32[1536,64]{1,0:T(8,128)}), f32[1536,64]{1,0:T(8,128)}) %all-reduce.3.cloned.1.call-update) | async-done | bytes 393232 | tf_op jit(solution)/shard_map/psum | solution.py:77
  313.8 1.6 fusion.35
  315.4 0.5 convolution_multiply_fusion
  315.9 0.2 copy.57
  316.2 2.5 gather_fusion.4
  318.6 0.2 copy.58
  318.9 0.3 gather.31
  319.2 0.3 slice_bitcast_fusion.3
  319.5 3.0 collective-permute-start.4
  322.5 1.3 collective-permute-start.7
  323.8 4.6 collective-permute-start.6
  328.4 2.8 collective-permute-start.5
  331.2 0.2 reshape.247
  331.5 77.0 %all-reduce = (f32[64]{0:T(128)S(1)}, f32[64]{0:T(128)S(1)}) all-reduce(f32[64]{0:T(128)S(1)} %get-tuple-element.31, f32[64]{0:T(128)S(1)} %get-tuple-element.30), channel_id=1, replica_groups=mesh['sub'=64,'grp'=4] {'sub','grp'}, use_global_device_ids=true, to_apply=%region_2.3 | all-reduce | flops 128 | bytes 1024 | tf_op jit(solution)/shard_map/psum | solution.py:77
  408.5 0.0 collective-permute-done.4
  408.5 0.0 collective-permute-done.7
  408.5 0.0 collective-permute-done.6
  408.5 0.0 collective-permute-done.5
  408.5 1.3 pad_maximum_fusion.1
  409.9 0.2 reshape.249
  410.1 0.2 reshape.248
  410.3 0.2 multiply_reduce_fusion
  410.5 73.4 %psum.31 = f32[64]{0:T(128)S(1)} all-reduce(f32[64]{0:T(128)S(1)} %broadcast_multiply_fusion.2), channel_id=1, replica_groups=mesh['sub'=64,'grp'=4] {'sub','grp'}, use_global_device_ids=true, to_apply=%region_8.9 | all-reduce | flops 64 | bytes 512 | tf_op jit(solution)/shard_map/psum | solution.py:84
  483.9 1.1 multiply_add_fusion
  (21 shorter events, 0.2 us)
Async XLA Ops:
  7.2 306.6 %copy-start = (f32[6,1536]{1,0:T(8,128)S(1)}, f32[6,1536]{1,0:T(8,128)}, u32[]{:S(2)}) copy-start(f32[6,1536]{1,0:T(8,128)} %param.13) | copy-start | bytes 110596
  7.2 306.6 %all-reduce.3.cloned.1.call-start = ((), (), s32[]{:S(2)}) async-start(), calls=%async_computation | async-start | bytes 1572864 | tf_op jit(solution)/shard_map/psum | solution.py:77
  25.2 29.1 %copy-start.2 = (f32[1,1,64,1200]{3,2,1,0:T(8,128)S(1)}, f32[1,1,64,1200]{3,2,1,0:T(8,128)}, u32[]{:S(2)}) copy-start(f32[1,1,64,1200]{3,2,1,0:T(8,128)} %param.10) | copy-start | bytes 921604
  25.2 29.1 %copy-start.3 = (f32[1,1,64,1200]{3,2,1,0:T(8,128)S(1)}, f32[1,1,64,1200]{3,2,1,0:T(8,128)}, u32[]{:S(2)}) copy-start(f32[1,1,64,1200]{3,2,1,0:T(8,128)} %param.9) | copy-start | bytes 921604
  34.1 23.1 %copy-start.5 = (f32[1,1,6,1200]{3,1,2,0:T(1,128)S(1)}, f32[1,1,6,1200]{3,1,2,0:T(1,128)}, u32[]{:S(2)}) copy-start(f32[1,1,6,1200]{3,1,2,0:T(1,128)} %param.12) | copy-start | bytes 86404
  37.5 12.5 %collective-permute-start = (f32[1,64,300]{2,0,1:T(1,128)S(1)}, f32[1,64,300]{2,0,1:T(1,128)S(1)}, u32[]{:S(2)}, u32[]{:S(2)}) collective-permute-start(f32[1,64,300]{2,0,1:T(1,128)S(1)} %get-tuple-element.24), channel_id=1, source_target_pairs={{0,4},{4,8},{8,12},{12,16},{16,20},{20,24},{24,28},{28,32},{32,36}... | collective-permute-start | bytes 230408 | tf_op jit(solution)/shard_map/ppermute | solution.py:12
  42.4 7.6 %collective-permute-start.3 = (f32[1,64,300]{2,0,1:T(1,128)S(1)}, f32[1,64,300]{2,0,1:T(1,128)S(1)}, u32[]{:S(2)}, u32[]{:S(2)}) collective-permute-start(f32[1,64,300]{2,0,1:T(1,128)S(1)} %get-tuple-element.25), channel_id=1, source_target_pairs={{1,0},{2,1},{3,2},{5,4},{6,5},{7,6},{9,8},{10,9},{11,10},{13,12},{... | collective-permute-start | bytes 230408 | tf_op jit(solution)/shard_map/ppermute | solution.py:15
  43.7 6.3 %collective-permute-start.2 = (f32[1,64,300]{2,0,1:T(1,128)S(1)}, f32[1,64,300]{2,0,1:T(1,128)S(1)}, u32[]{:S(2)}, u32[]{:S(2)}) collective-permute-start(f32[1,64,300]{2,0,1:T(1,128)S(1)} %get-tuple-element.26), channel_id=1, source_target_pairs={{0,1},{1,2},{2,3},{4,5},{5,6},{6,7},{8,9},{9,10},{10,11},{12,13},{... | collective-permute-start | bytes 230408 | tf_op jit(solution)/shard_map/ppermute | solution.py:12
  47.7 5.9 %collective-permute-start.1 = (f32[1,64,300]{2,0,1:T(1,128)S(1)}, f32[1,64,300]{2,0,1:T(1,128)S(1)}, u32[]{:S(2)}, u32[]{:S(2)}) collective-permute-start(f32[1,64,300]{2,0,1:T(1,128)S(1)} %get-tuple-element.27), channel_id=1, source_target_pairs={{4,0},{8,4},{12,8},{16,12},{20,16},{24,20},{28,24},{32,28},{36,32}... | collective-permute-start | bytes 230408 | tf_op jit(solution)/shard_map/ppermute | solution.py:15
  58.0 0.9 copy-start.1
  58.9 425.0 %copy-start.4 = (f32[1,1,64,1200]{3,2,1,0:T(8,128)S(1)}, f32[1,1,64,1200]{3,2,1,0:T(8,128)}, u32[]{:S(2)}) copy-start(f32[1,1,64,1200]{3,2,1,0:T(8,128)} %param.8) | copy-start | bytes 921604
  319.5 89.0 %collective-permute-start.4 = (f32[1,64,300]{2,0,1:T(1,128)S(1)}, f32[1,64,300]{2,0,1:T(1,128)S(1)}, u32[]{:S(2)}, u32[]{:S(2)}) collective-permute-start(f32[1,64,300]{2,0,1:T(1,128)S(1)} %get-tuple-element.20), channel_id=1, source_target_pairs={{0,4},{4,8},{8,12},{12,16},{16,20},{20,24},{24,28},{28,32},{32,36}... | collective-permute-start | bytes 230408 | tf_op jit(solution)/shard_map/ppermute | solution.py:12
  322.5 86.0 %collective-permute-start.7 = (f32[1,64,300]{2,0,1:T(1,128)S(1)}, f32[1,64,300]{2,0,1:T(1,128)S(1)}, u32[]{:S(2)}, u32[]{:S(2)}) collective-permute-start(f32[1,64,300]{2,0,1:T(1,128)S(1)} %get-tuple-element.21), channel_id=1, source_target_pairs={{1,0},{2,1},{3,2},{5,4},{6,5},{7,6},{9,8},{10,9},{11,10},{13,12},{... | collective-permute-start | bytes 230408 | tf_op jit(solution)/shard_map/ppermute | solution.py:15
  323.8 84.7 %collective-permute-start.6 = (f32[1,64,300]{2,0,1:T(1,128)S(1)}, f32[1,64,300]{2,0,1:T(1,128)}, u32[]{:S(2)}, u32[]{:S(2)}) collective-permute-start(f32[1,64,300]{2,0,1:T(1,128)S(1)} %get-tuple-element.22), channel_id=1, source_target_pairs={{0,1},{1,2},{2,3},{4,5},{5,6},{6,7},{8,9},{9,10},{10,11},{12,13},{... | collective-permute-start | bytes 230408 | tf_op jit(solution)/shard_map/ppermute | solution.py:12
  328.4 80.1 %collective-permute-start.5 = (f32[1,64,300]{2,0,1:T(1,128)S(1)}, f32[1,64,300]{2,0,1:T(1,128)}, u32[]{:S(2)}, u32[]{:S(2)}) collective-permute-start(f32[1,64,300]{2,0,1:T(1,128)S(1)} %get-tuple-element.23), channel_id=1, source_target_pairs={{4,0},{8,4},{12,8},{16,12},{20,16},{24,20},{28,24},{32,28},{36,32}... | collective-permute-start | bytes 230408 | tf_op jit(solution)/shard_map/ppermute | solution.py:15
Sparse Core Ops, SparseCore 0:
  59.0 254.7 all-reduce.2
where the time goes:
time: 493 us; the launch traced here: 492 us
  waiting for transfers between devices  259 us (53%)
  blocking collectives  150 us (30%)
  starting transfers between devices  24.2 us (5%)
  local copies, waits for them, and re-layouts  21.2 us (4%)
  between operations  14.5 us (3%)
  other arithmetic  11.7 us (2%)
  matrix products  11.3 us (2%)
    psum x1, waiting for transfers between devices, on_device(): lax.psum((dense, rr_local, curv_local), ('sub', 'grp'))  255 us
    psum x1, blocking collectives, on_device(): lax.psum((dense, rr_local, curv_local), ('sub', 'grp'))  77 us
    psum x1, blocking collectives, on_device(): lax.psum(0.5 * jnp.sum(res_next * res_next, axis=1), ('sub', 'grp'))  73.4 us
    ppermute x4, starting transfers between devices, with_halo(): lax.ppermute(lax.slice_in_dim(block, block.shape[dim] - width, None, axis...  16.5 us
  transfers between devices with their start and end apart: 9, of which 2 were waited for; matrix products, arithmetic and copies ran while one was open for 0% of the time, Pallas kernels for 0%

commit v1 on v0

v1 whole, which is shorter than its diff:
```python
import functools

import jax
import jax.numpy as jnp
from jax import lax
from jax.experimental import pallas as pl
from jax.experimental.pallas import tpu as pltpu
from jax.sharding import PartitionSpec as P

MESH = pl.DeviceIdType.MESH
F32 = jnp.float32
BF16 = jnp.bfloat16
NN = (((1,), (0,)), ((), ()))
NT = (((1,), (1,)), ((), ()))
TN = (((0,), (0,)), ((), ()))

CASES = 64
WIDTH = 1200
FACE = 300
PAD = 384
WIDE = 4 * PAD
MODES = 6
COARSE = 1536
WINDOW = 256
MEMBERS = 16


def split(x):
    high = x.astype(BF16)
    return high, (x - high.astype(F32)).astype(BF16)


def mm(a, b, dims):
    return lax.dot_general(a, b, dims, preferred_element_type=F32)


def iota(shape, dim):
    return lax.broadcasted_iota(jnp.int32, shape, dim)


def face_at(lane, step):
    one = jnp.int32(1)
    zero = jnp.int32(0)
    return (
        jnp.where(lane >= step, one, zero)
        + jnp.where(lane >= 2 * step, one, zero)
        + jnp.where(lane >= 3 * step, one, zero)
    )


def row_of(column):
    eye = iota((CASES, 128), 0) == iota((CASES, 128), 1)
    return jnp.sum(jnp.where(eye, column, 0.0), axis=0, keepdims=True)


def column_of(row):
    eye = iota((CASES, 128), 0) == iota((CASES, 128), 1)
    return jnp.sum(jnp.where(eye, row, 0.0), axis=1, keepdims=True)


def window_start(block):
    return min(max(((96 * block - 24) // 128) * 128, 0), COARSE - WINDOW)


def kernel(
    lam_hbm,
    res_hbm,
    dir_hbm,
    dual_hbm,
    trace_hbm,
    inv_hbm,
    sizes_ref,
    order_ref,
    lam_out,
    res_out,
    dir_out,
    lam_v,
    res_v,
    dir_v,
    dual_v,
    trace_v,
    inv_v,
    inv_pad,
    perm,
    own_rf,
    nb_rf,
    own_y,
    nb_y,
    windows,
    loads,
    parts,
    got,
    amps,
    norm_a,
    norm_b,
    in_sem,
    out_sem,
    send_sem,
    recv_sem,
):
    s = lax.axis_index("sub")
    g = lax.axis_index("grp")
    block = s // 4
    sl = s % 4
    place = sl * 4 + g

    copies_in = {}
    for k, (name, src, dst) in enumerate(
        (
            ("dir", dir_hbm, dir_v),
            ("trace", trace_hbm, trace_v),
            ("inv", inv_hbm, inv_v),
            ("dual", dual_hbm, dual_v),
            ("res", res_hbm, res_v),
            ("lam", lam_hbm, lam_v),
        )
    ):
        copies_in[name] = pltpu.make_async_copy(src, dst, in_sem.at[k])
        copies_in[name].start()

    across = (
        ((s + 63) % 64, g),
        ((s + 1) % 64, g),
        (s, (g + 3) % 4),
        (s, (g + 1) % 4),
    )

    def mate(step):
        other = (place + step) % MEMBERS
        return (block * 4 + other // 4, other % 4)

    def peer(step):
        other = (block + step) % MEMBERS
        return other, (other * 4 + sl, g)

    barrier = pltpu.get_barrier_semaphore()
    for target in across:
        pl.semaphore_signal(barrier, inc=1, device_id=target, device_id_type=MESH)
    for step in range(1, MEMBERS):
        pl.semaphore_signal(barrier, inc=1, device_id=mate(step), device_id_type=MESH)
        pl.semaphore_signal(barrier, inc=1, device_id=peer(step)[1], device_id_type=MESH)

    def send(src, dst, phase, target):
        pltpu.make_async_remote_copy(
            src_ref=src,
            dst_ref=dst,
            send_sem=send_sem.at[phase],
            recv_sem=recv_sem.at[phase],
            device_id=target,
            device_id_type=MESH,
        ).start()

    def wait_recv(ref, phase):
        pltpu.make_async_copy(ref, ref, recv_sem.at[phase]).wait()

    def wait_send(ref, phase):
        pltpu.make_async_copy(ref, ref, send_sem.at[phase]).wait()

    def limits(face):
        out = jnp.zeros_like(face)
        for f in range(4):
            out = jnp.where(face == f, sizes_ref[0, 0, f], out)
        return out

    lane = iota((1, WIDE), 1)
    face = face_at(lane, PAD)
    active_pad = (lane - face * PAD) < limits(face)
    sign_pad = jnp.where((face & 1) == 0, -1.0, 1.0)
    mask_pad = jnp.where(active_pad, sign_pad, 0.0)
    flat = iota((1, WIDTH), 1)
    flat_face = face_at(flat, FACE)
    active = (flat - flat_face * FACE) < limits(flat_face)

    order = order_ref[0]
    order = order + (PAD - FACE) * face_at(order, FACE)
    for f in range(4):
        hot = iota((PAD, WIDTH), 0) + f * PAD == order
        perm[f * PAD : (f + 1) * PAD, :] = jnp.where(hot, 1.0, 0.0).astype(BF16)

    copies_in["trace"].wait()
    trace = jnp.concatenate([trace_v[...], jnp.zeros((2, WIDTH), F32)], axis=0)
    high, low = split(trace)
    both = jnp.concatenate([high.astype(F32), low.astype(F32)], axis=0).astype(BF16)
    for f in range(4):
        got_rf = mm(both, perm[f * PAD : (f + 1) * PAD, :], NT)
        own_rf[f] = (got_rf[:8] + got_rf[8:]) * mask_pad[:, f * PAD : (f + 1) * PAD]
    copies_in["inv"].wait()
    inv_pad[...] = jnp.concatenate([inv_v[...], jnp.zeros((2, COARSE), F32)], axis=0)

    pl.semaphore_wait(barrier, 34)
    for f in range(4):
        send(own_rf.at[f], nb_rf.at[f ^ 1], 0, across[f])
    for b in range(MEMBERS):
        piece = inv_pad.at[:, window_start(b) : window_start(b) + WINDOW]

        @pl.when(block != b)
        def _():
            send(piece, windows.at[block], 1, (b * 4 + sl, g))

        @pl.when(block == b)
        def _():
            windows[b] = piece[...]

    copies_in["dir"].wait()
    direction = dir_v[...]
    gap = jnp.zeros((CASES, PAD - FACE), F32)
    spread = []
    for f in range(4):
        spread += [direction[:, f * FACE : (f + 1) * FACE], gap]
    spread = jnp.concatenate(spread, axis=1)
    spread = jnp.where(active_pad, spread * sign_pad, 0.0)
    high, low = split(spread)
    slots = mm(jnp.concatenate([high, low], axis=0), perm[...], NN)
    slots = slots[:CASES] + slots[CASES:]

    high, low = split(slots)
    both = jnp.concatenate([high, low], axis=0)
    copies_in["dual"].wait()
    pieces = []
    for k in range(0, WIDTH, 256):
        f_high, f_low = split(dual_v[k : min(k + 256, WIDTH), :])
        first = mm(both, f_high, NT)
        pieces.append(first[:CASES] + first[CASES:] + mm(high, f_low, NT))
    z = jnp.concatenate(pieces, axis=1)

    high, low = split(z)
    both = jnp.concatenate([high, low], axis=0)
    wait_recv(nb_rf, 0)
    own_load = jnp.zeros((8, 128), F32)
    for f in range(4):
        cut = slice(f * PAD, (f + 1) * PAD)
        y = mm(both, perm[cut, :], NT)
        y = (y[:CASES] + y[CASES:]) * mask_pad[:, cut]
        own_y[f] = y
        nb_rf[f] = jnp.where(active_pad[:, cut], nb_rf[f], 0.0)
        rf = jnp.concatenate([own_rf[f], nb_rf[f]], axis=0)
        r_high, r_low = split(rf)
        y_high, y_low = split(y)
        piece = mm(
            jnp.concatenate([r_high, r_low], axis=0), jnp.concatenate([y_high, y_low], axis=0), NT
        )
        piece = piece[:16] + piece[16:]
        piece = piece + pltpu.roll(piece, 64, 1)
        own_load = own_load + piece[:8]
        loads[place, 8 * (f + 1) : 8 * (f + 2), :] = piece[8:]

    copies_in["res"].wait()
    res = jnp.where(active, res_v[...], 0.0)
    rr_row = row_of(0.5 * jnp.sum(res * res, axis=1, keepdims=True))
    curv_row = row_of(jnp.sum(slots * z, axis=1, keepdims=True))
    row = iota((8, 128), 0)
    own_load = jnp.where(row == 6, rr_row, jnp.where(row == 7, curv_row, own_load))
    loads[place, 0:8, :] = own_load
    for step in range(1, MEMBERS):
        send(loads.at[place], loads.at[place], 2, mate(step))
    for f in range(4):
        send(own_y.at[f], nb_y.at[f ^ 1], 3, across[f])

    col = iota((1, 40 * MEMBERS), 1)
    unit = col >> 3
    mode = col & 7
    member = (unit * 205) >> 10
    group = unit - member * 5
    d_sub = jnp.where(group == 1, -1, jnp.where(group == 2, 1, 0))
    d_grp = jnp.where(group == 3, -1, jnp.where(group == 4, 1, 0))
    m_sub = block * 4 + (member >> 2) + d_sub
    m_grp = (member & 3) + d_grp
    start = jnp.clip(((96 * block + 104) // 128 - 1) * 128, 0, COARSE - WINDOW)
    source = (m_sub * 4 + m_grp) * MODES + mode - start
    source = jnp.where(mode < MODES, source, -1)
    pick = jnp.where(iota((WINDOW, 40 * MEMBERS), 0) == source, 1.0, 0.0).astype(BF16)
    wait_recv(windows.at[0 : MEMBERS - 1], 1)
    high, low = split(windows[...].reshape(MEMBERS * 8, WINDOW))
    piece = mm(jnp.concatenate([high, low], axis=0), pick, NN).astype(BF16)

    wait_recv(loads.at[0 : MEMBERS - 1], 2)
    every = loads[...]
    total = jnp.sum(every[:, 0:8, :], axis=0)
    flat_load = every.reshape(MEMBERS * 40, 128)
    high = flat_load.astype(BF16)
    low = (flat_load - high.astype(F32)).astype(BF16)
    both = jnp.where(iota((MEMBERS * 40, 128), 1) < 64, high.astype(F32), low.astype(F32)).astype(BF16)
    part = mm(piece, both, NN)
    part = part[:128] + part[128:]
    part = part + pltpu.roll(part, 64, 1)
    part = part.reshape(MEMBERS, 8, 128)
    parts[...] = part + jnp.where(row >= 6, total, 0.0)[None]
    for step in range(1, MEMBERS):
        other, target = peer(step)
        send(parts.at[other], got.at[block], 4, target)
    got[block] = parts[block]
    wait_recv(got.at[0 : MEMBERS - 1], 4)
    amp = jnp.sum(got[...], axis=0)
    amps[0] = amp
    for f in range(4):
        send(amps.at[0], amps.at[1 + (f ^ 1)], 5, across[f])

    rr = column_of(amp[6:7, :])
    curvature = column_of(amp[7:8, :])
    step_size = rr / curvature
    dirn = jnp.where(active, dir_v[...], 0.0)
    copies_in["lam"].wait()
    lam_v[...] = jnp.where(active, lam_v[...], 0.0) + step_size * dirn
    lam_copy = pltpu.make_async_copy(lam_v, lam_out, out_sem.at[0])
    lam_copy.start()

    wait_recv(nb_y, 3)
    wait_recv(amps.at[1:5], 5)
    spread = []
    for f in range(4):
        cut = slice(f * PAD, (f + 1) * PAD)
        a_high, a_low = split(jnp.concatenate([amp, amps[1 + f]], axis=0))
        r_high, r_low = split(jnp.concatenate([own_rf[f], nb_rf[f]], axis=0))
        back = mm(
            jnp.concatenate([a_high, a_low, a_high, a_low], axis=0),
            jnp.concatenate([r_high, r_high, r_low, r_low], axis=0),
            TN,
        )
        image = own_y[f] + jnp.where(active_pad[:, cut], nb_y[f], 0.0)
        spread.append((image - back[:CASES])[:, :FACE])
    projected = jnp.concatenate(spread, axis=1)
    res = jnp.where(active, res_v[...], 0.0) - step_size * projected
    res_v[...] = res
    res_copy = pltpu.make_async_copy(res_v, res_out, out_sem.at[1])
    res_copy.start()

    next_row = row_of(0.5 * jnp.sum(res * res, axis=1, keepdims=True))
    norm_a[place] = jnp.broadcast_to(next_row, (8, 128))
    for step in range(1, MEMBERS):
        send(norm_a.at[place], norm_a.at[place], 6, mate(step))
    wait_recv(norm_a.at[0 : MEMBERS - 1], 6)
    norm_b[block] = jnp.sum(norm_a[...], axis=0)
    for step in range(1, MEMBERS):
        send(norm_b.at[block], norm_b.at[block], 7, peer(step)[1])
    wait_recv(norm_b.at[0 : MEMBERS - 1], 7)
    rr_next = column_of(jnp.sum(norm_b[...], axis=0)[0:1, :])
    dir_v[...] = res + (rr_next / rr) * dirn
    dir_copy = pltpu.make_async_copy(dir_v, dir_out, out_sem.at[2])
    dir_copy.start()

    wait_send(own_rf, 0)
    wait_send(windows.at[0 : MEMBERS - 1], 1)
    wait_send(loads.at[0 : MEMBERS - 1], 2)
    wait_send(own_y, 3)
    wait_send(parts.at[0 : MEMBERS - 1], 4)
    wait_send(amps.at[1:5], 5)
    wait_send(norm_a.at[0 : MEMBERS - 1], 6)
    wait_send(norm_b.at[0 : MEMBERS - 1], 7)
    lam_copy.wait()
    res_copy.wait()
    dir_copy.wait()


def on_device(
    multipliers,
    residual,
    direction,
    dual_operator,
    rigid_trace,
    coarse_inverse,
    face_sizes,
    slot_order,
):
    field = jax.ShapeDtypeStruct((CASES, WIDTH), F32)
    anywhere = pl.BlockSpec(memory_space=pl.ANY)
    outs = pl.pallas_call(
        kernel,
        out_shape=(field, field, field),
        in_specs=[anywhere] * 6
        + [pl.BlockSpec(memory_space=pltpu.SMEM), pl.BlockSpec(memory_space=pltpu.VMEM)],
        out_specs=(anywhere, anywhere, anywhere),
        scratch_shapes=[
            pltpu.VMEM((CASES, WIDTH), F32),
            pltpu.VMEM((CASES, WIDTH), F32),
            pltpu.VMEM((CASES, WIDTH), F32),
            pltpu.VMEM((WIDTH, WIDTH), F32),
            pltpu.VMEM((MODES, WIDTH), F32),
            pltpu.VMEM((MODES, COARSE), F32),
            pltpu.VMEM((8, COARSE), F32),
            pltpu.VMEM((WIDE, WIDTH), BF16),
            pltpu.VMEM((4, 8, PAD), F32),
            pltpu.VMEM((4, 8, PAD), F32),
            pltpu.VMEM((4, CASES, PAD), F32),
            pltpu.VMEM((4, CASES, PAD), F32),
            pltpu.VMEM((MEMBERS, 8, WINDOW), F32),
            pltpu.VMEM((MEMBERS, 40, 128), F32),
            pltpu.VMEM((MEMBERS, 8, 128), F32),
            pltpu.VMEM((MEMBERS, 8, 128), F32),
            pltpu.VMEM((5, 8, 128), F32),
            pltpu.VMEM((MEMBERS, 8, 128), F32),
            pltpu.VMEM((MEMBERS, 8, 128), F32),
            pltpu.SemaphoreType.DMA((6,)),
            pltpu.SemaphoreType.DMA((3,)),
            pltpu.SemaphoreType.DMA((8,)),
            pltpu.SemaphoreType.DMA((8,)),
        ],
        compiler_params=pltpu.CompilerParams(
            collective_id=0, has_side_effects=True, vmem_limit_bytes=48 * 1024 * 1024
        ),
    )(
        multipliers.reshape(CASES, WIDTH),
        residual.reshape(CASES, WIDTH),
        direction.reshape(CASES, WIDTH),
        dual_operator.reshape(WIDTH, WIDTH),
        rigid_trace.reshape(MODES, WIDTH),
        coarse_inverse,
        face_sizes,
        slot_order,
    )
    return tuple(x[None, None] for x in outs)


def solution(mesh):
    wide = P("sub", "grp", None, None)
    return jax.shard_map(
        on_device,
        mesh=mesh,
        in_specs=(wide, wide, wide, wide, wide, P(("sub", "grp"), None), P("sub", "grp", None), P("sub", "grp", None)),
        out_specs=(wide, wide, wide),
        check_vma=False,
    )
```

time: 493 us -> 53.8 us (0.11)
  waiting for transfers between devices: 259 us -> 0 us
  blocking collectives: 150 us -> 0 us
  Pallas kernels: 0 us -> 44.8 us
  starting transfers between devices: 24.2 us -> 0 us
  between operations: 14.5 us -> 0.65 us
  local copies, waits for them, and re-layouts: 21.2 us -> 7.99 us
  other arithmetic: 11.7 us -> 0 us
  matrix products: 11.3 us -> 0 us
    psum x1 -> x0, waiting for transfers between devices: 255 us -> none  [on_device(): lax.psum((dense, rr_local, curv_local), ('sub', 'grp'))]
    psum x2 -> x0, blocking collectives: 150 us -> none  [the longest x1 77 us: on_device(): lax.psum((dense, rr_local, curv_local), ('sub', 'grp'))]
    pallas_call x0 -> x1, Pallas kernels: none -> 44.8 us  [on_device(): pl.pallas_call(kernel, out_shape=(field, field, field), in_specs=[anywher...]
    ppermute x8 -> x0, starting transfers between devices: 24.2 us -> none  [the longest x4 16.5 us: with_halo(): lax.ppermute(lax.slice_in_dim(block, block.shape[dim] - width, None, axis...]
    gather x9 -> x0, local copies, waits for them, and re-layouts: 17.7 us -> none  [the longest x1 6.78 us: on_device(): slot_sign = face_sign[order][None, :]]
    dot_general x4 -> x0, matrix products: 11.3 us -> none  [the longest x1 8.65 us: on_device(): lax.dot_general(to_slots(dirn), dual, (((1,), (1,)), ((), ())), precision...]
    unnamed x14 -> x16, local copies, waits for them, and re-layouts: 0.94 us -> 7.99 us
    sort x1 -> x0, other arithmetic: 5.11 us -> none  [on_device(): inverse = jnp.argsort(order)]
  transfers between devices with their start and end apart: 9 -> 0, of which waited for: 2 -> 0; matrix products, arithmetic and copies ran while one was open for 0% -> 0% of each run, Pallas kernels for 0% -> 0%
where the time goes in v1:
time: 53.8 us; the launch traced here: 53.4 us
  Pallas kernels  44.8 us (83%)
  local copies, waits for them, and re-layouts  7.99 us (15%)
  between operations  0.65 us (1%)
    pallas_call x1, Pallas kernels, on_device(): pl.pallas_call(kernel, out_shape=(field, field, field), in_specs=[anywher...  44.8 us
    unnamed x16, local copies, waits for them, and re-layouts  7.99 us

profile of v1, /device:TPU:1, one launch (start us, length us, event | category | flops | bytes accessed | tf_op | source)
XLA Modules:
  0.0 53.4 jit_solution(14638567741880126523)
XLA Ops:
  0.6 0.8 %copy.13 = f32[1,1,6,1200]{3,2,1,0:T(8,128)S(1)} copy(f32[1,1,6,1200]{3,1,2,0:T(1,128)} %param.12) | data formatting | bytes 57600
  1.4 0.0 copy-start
  1.4 1.0 %copy-done = f32[1,1,64,1200]{3,2,1,0:T(8,128)S(1)} copy-done((f32[1,1,64,1200]{3,2,1,0:T(8,128)S(1)}, f32[1,1,64,1200]{3,2,1,0:T(8,128)}, u32[]{:S(2)}) %copy-start) | copy-done | bytes 307224
  2.4 0.0 copy-start.1
  2.4 1.0 %copy-done.1 = f32[1,1,64,1200]{3,2,1,0:T(8,128)S(1)} copy-done((f32[1,1,64,1200]{3,2,1,0:T(8,128)S(1)}, f32[1,1,64,1200]{3,2,1,0:T(8,128)}, u32[]{:S(2)}) %copy-start.1) | copy-done | bytes 307224
  3.3 0.0 copy-start.2
  3.3 1.0 %copy-done.2 = f32[1,1,64,1200]{3,2,1,0:T(8,128)S(1)} copy-done((f32[1,1,64,1200]{3,2,1,0:T(8,128)S(1)}, f32[1,1,64,1200]{3,2,1,0:T(8,128)}, u32[]{:S(2)}) %copy-start.2) | copy-done | bytes 307224
  4.3 0.0 copy-start.3
  4.3 0.8 %copy-done.3 = f32[6,1536]{1,0:T(8,128)S(1)} copy-done((f32[6,1536]{1,0:T(8,128)S(1)}, f32[6,1536]{1,0:T(8,128)}, u32[]{:S(2)}) %copy-start.3) | copy-done | bytes 36888
  5.1 0.0 copy-start.4
  5.1 0.7 %copy-done.4 = s32[1,1,1200]{2,1,0:T(1,128)S(1)} copy-done((s32[1,1,1200]{2,1,0:T(1,128)S(1)}, s32[1,1,1200]{2,1,0:T(1,128)}, u32[]{:S(2)}) %copy-start.4) | copy-done | bytes 4824
  5.8 0.0 copy-start.5
  5.8 0.7 %copy-done.5 = s32[1,1,4]{2,1,0:T(1,128)S(1)} copy-done((s32[1,1,4]{2,1,0:T(1,128)S(1)}, s32[1,1,4]{2,1,0:T(1,128)}, u32[]{:S(2)}) %copy-start.5) | copy-done | bytes 40
  6.5 44.8 %shard_map.103 = (f32[64,1200]{1,0:T(8,128)S(1)}, f32[64,1200]{1,0:T(8,128)S(1)}, f32[64,1200]{1,0:T(8,128)S(1)}) custom-call(f32[64,1200]{1,0:T(8,128)S(1)} %bitcast.10, f32[64,1200]{1,0:T(8,128)S(1)} %bitcast.11, f32[64,1200]{1,0:T(8,128)S(1)} %bitcast.12, f32[1200,1200]{1,0:T(8,128)} %bitcast.17, f32[6,1200]{1,0:T(8,128)S(1)} %bitcast.16, ...), custom_call_target="tpu_custom_call" | custom-call | tf_op jit(solution)/shard_map/pallas_call | solution.py:366
  51.3 0.7 %copy.17 = f32[1,1,64,1200]{3,2,1,0:T(8,128)} copy(f32[1,1,64,1200]{3,2,1,0:T(8,128)S(1)} %bitcast.15) | data formatting | bytes 614400
  52.0 0.7 %copy.18 = f32[1,1,64,1200]{3,2,1,0:T(8,128)} copy(f32[1,1,64,1200]{3,2,1,0:T(8,128)S(1)} %bitcast.14) | data formatting | bytes 614400
  52.7 0.7 %copy.19 = f32[1,1,64,1200]{3,2,1,0:T(8,128)} copy(f32[1,1,64,1200]{3,2,1,0:T(8,128)S(1)} %bitcast.13) | data formatting | bytes 614400
Async XLA Ops:
  1.4 1.0 %copy-start = (f32[1,1,64,1200]{3,2,1,0:T(8,128)S(1)}, f32[1,1,64,1200]{3,2,1,0:T(8,128)}, u32[]{:S(2)}) copy-start(f32[1,1,64,1200]{3,2,1,0:T(8,128)} %param.8) | copy-start | bytes 921604
  2.4 1.0 %copy-start.1 = (f32[1,1,64,1200]{3,2,1,0:T(8,128)S(1)}, f32[1,1,64,1200]{3,2,1,0:T(8,128)}, u32[]{:S(2)}) copy-start(f32[1,1,64,1200]{3,2,1,0:T(8,128)} %param.9) | copy-start | bytes 921604
  3.3 1.0 %copy-start.2 = (f32[1,1,64,1200]{3,2,1,0:T(8,128)S(1)}, f32[1,1,64,1200]{3,2,1,0:T(8,128)}, u32[]{:S(2)}) copy-start(f32[1,1,64,1200]{3,2,1,0:T(8,128)} %param.10) | copy-start | bytes 921604
  4.3 0.8 %copy-start.3 = (f32[6,1536]{1,0:T(8,128)S(1)}, f32[6,1536]{1,0:T(8,128)}, u32[]{:S(2)}) copy-start(f32[6,1536]{1,0:T(8,128)} %inv_hbm.1) | copy-start | bytes 110596
  5.1 0.7 %copy-start.4 = (s32[1,1,1200]{2,1,0:T(1,128)S(1)}, s32[1,1,1200]{2,1,0:T(1,128)}, u32[]{:S(2)}) copy-start(s32[1,1,1200]{2,1,0:T(1,128)} %order_ref.1) | copy-start | bytes 14404
  5.8 0.7 %copy-start.5 = (s32[1,1,4]{2,1,0:T(1,128)S(1)}, s32[1,1,4]{2,1,0:T(1,128)}, u32[]{:S(2)}) copy-start(s32[1,1,4]{2,1,0:T(1,128)} %sizes_ref.1) | copy-start | bytes 52

commit v2 on v1

--- a/solution.py
+++ b/solution.py
@@ -63,23 +63,23 @@
 
 
 def kernel(
-    lam_hbm,
     res_hbm,
     dir_hbm,
     dual_hbm,
     trace_hbm,
     inv_hbm,
-    sizes_ref,
-    order_ref,
-    lam_out,
-    res_out,
-    dir_out,
-    lam_v,
+    sizes_hbm,
+    order_hbm,
+    proj_out,
+    coef_out,
+    proj_v,
     res_v,
     dir_v,
     dual_v,
     trace_v,
     inv_v,
+    order_ref,
+    sizes_ref,
     inv_pad,
     perm,
     own_rf,
@@ -107,12 +107,13 @@
     copies_in = {}
     for k, (name, src, dst) in enumerate(
         (
+            ("sizes", sizes_hbm, sizes_ref),
+            ("order", order_hbm, order_ref),
+            ("trace", trace_hbm, trace_v),
             ("dir", dir_hbm, dir_v),
-            ("trace", trace_hbm, trace_v),
             ("inv", inv_hbm, inv_v),
             ("dual", dual_hbm, dual_v),
             ("res", res_hbm, res_v),
-            ("lam", lam_hbm, lam_v),
         )
     ):
         copies_in[name] = pltpu.make_async_copy(src, dst, in_sem.at[k])
@@ -156,6 +157,24 @@
     def wait_send(ref, phase):
         pltpu.make_async_copy(ref, ref, send_sem.at[phase]).wait()
 
+    def greeted():
+        pl.semaphore_wait(barrier, 34)
+        for f in range(4):
+            send(own_rf.at[f], nb_rf.at[f ^ 1], 0, across[f])
+        for b in range(MEMBERS):
+            piece = inv_pad.at[:, window_start(b) : window_start(b) + WINDOW]
+
+            @pl.when(block != b)
+            def _():
+                send(piece, windows.at[block], 1, (b * 4 + sl, g))
+
+            @pl.when(block == b)
+            def _():
+                windows[b] = piece[...]
+
+    copies_in["sizes"].wait()
+    copies_in["order"].wait()
+
     def limits(face):
         out = jnp.zeros_like(face)
         for f in range(4):
@@ -178,7 +197,7 @@
         perm[f * PAD : (f + 1) * PAD, :] = jnp.where(hot, 1.0, 0.0).astype(BF16)
 
     copies_in["trace"].wait()
-    trace = jnp.concatenate([trace_v[...], jnp.zeros((2, WIDTH), F32)], axis=0)
+    trace = jnp.concatenate([trace_v[...].reshape(MODES, WIDTH), jnp.zeros((2, WIDTH), F32)], axis=0)
     high, low = split(trace)
     both = jnp.concatenate([high.astype(F32), low.astype(F32)], axis=0).astype(BF16)
     for f in range(4):
@@ -186,20 +205,6 @@
         own_rf[f] = (got_rf[:8] + got_rf[8:]) * mask_pad[:, f * PAD : (f + 1) * PAD]
     copies_in["inv"].wait()
     inv_pad[...] = jnp.concatenate([inv_v[...], jnp.zeros((2, COARSE), F32)], axis=0)
-
-    pl.semaphore_wait(barrier, 34)
-    for f in range(4):
-        send(own_rf.at[f], nb_rf.at[f ^ 1], 0, across[f])
-    for b in range(MEMBERS):
-        piece = inv_pad.at[:, window_start(b) : window_start(b) + WINDOW]
-
-        @pl.when(block != b)
-        def _():
-            send(piece, windows.at[block], 1, (b * 4 + sl, g))
-
-        @pl.when(block == b)
-        def _():
-            windows[b] = piece[...]
 
     copies_in["dir"].wait()
     direction = dir_v[...]
@@ -218,6 +223,8 @@
     copies_in["dual"].wait()
     pieces = []
     for k in range(0, WIDTH, 256):
+        if k == 512:
+            greeted()
         f_high, f_low = split(dual_v[k : min(k + 256, WIDTH), :])
         first = mm(both, f_high, NT)
         pieces.append(first[:CASES] + first[CASES:] + mm(high, f_low, NT))
@@ -225,42 +232,49 @@
 
     high, low = split(z)
     both = jnp.concatenate([high, low], axis=0)
+    for f in range(4):
+        cut = slice(f * PAD, (f + 1) * PAD)
+        y = mm(both, perm[cut, :], NT)
+        own_y[f] = (y[:CASES] + y[CASES:]) * mask_pad[:, cut]
     wait_recv(nb_rf, 0)
     own_load = jnp.zeros((8, 128), F32)
+    nb_load = []
     for f in range(4):
         cut = slice(f * PAD, (f + 1) * PAD)
-        y = mm(both, perm[cut, :], NT)
-        y = (y[:CASES] + y[CASES:]) * mask_pad[:, cut]
-        own_y[f] = y
         nb_rf[f] = jnp.where(active_pad[:, cut], nb_rf[f], 0.0)
-        rf = jnp.concatenate([own_rf[f], nb_rf[f]], axis=0)
-        r_high, r_low = split(rf)
-        y_high, y_low = split(y)
+        r_high, r_low = split(jnp.concatenate([own_rf[f], nb_rf[f]], axis=0))
+        y_high, y_low = split(own_y[f])
         piece = mm(
             jnp.concatenate([r_high, r_low], axis=0), jnp.concatenate([y_high, y_low], axis=0), NT
         )
         piece = piece[:16] + piece[16:]
         piece = piece + pltpu.roll(piece, 64, 1)
         own_load = own_load + piece[:8]
-        loads[place, 8 * (f + 1) : 8 * (f + 2), :] = piece[8:]
-
+        nb_load.append(piece[8:])
     copies_in["res"].wait()
     res = jnp.where(active, res_v[...], 0.0)
     rr_row = row_of(0.5 * jnp.sum(res * res, axis=1, keepdims=True))
     curv_row = row_of(jnp.sum(slots * z, axis=1, keepdims=True))
     row = iota((8, 128), 0)
+    left = iota((8, 128), 1) < 64
     own_load = jnp.where(row == 6, rr_row, jnp.where(row == 7, curv_row, own_load))
-    loads[place, 0:8, :] = own_load
+    for f in range(3):
+        moved = pltpu.roll(nb_load[3], 6 - 2 * f, 0)
+        nb_load[f] = jnp.where(row < MODES, nb_load[f], moved)
+    loads[place, 0:8, :] = jnp.where(left, own_load, nb_load[0])
+    loads[place, 8:16, :] = jnp.where(left, nb_load[1], nb_load[2])
     for step in range(1, MEMBERS):
         send(loads.at[place], loads.at[place], 2, mate(step))
     for f in range(4):
         send(own_y.at[f], nb_y.at[f ^ 1], 3, across[f])
 
-    col = iota((1, 40 * MEMBERS), 1)
-    unit = col >> 3
+    col = iota((1, 2 * WINDOW), 1)
     mode = col & 7
-    member = (unit * 205) >> 10
-    group = unit - member * 5
+    tile = 2 * ((col >> 3) & 1) + (col >> 8)
+    member = (col >> 4) & 15
+    spare = (mode >= MODES) & (tile > 0)
+    group = jnp.where(spare, 4, tile)
+    mode = jnp.where(spare, 2 * (tile - 1) + mode - MODES, mode)
     d_sub = jnp.where(group == 1, -1, jnp.where(group == 2, 1, 0))
     d_grp = jnp.where(group == 3, -1, jnp.where(group == 4, 1, 0))
     m_sub = block * 4 + (member >> 2) + d_sub
@@ -268,29 +282,33 @@
     start = jnp.clip(((96 * block + 104) // 128 - 1) * 128, 0, COARSE - WINDOW)
     source = (m_sub * 4 + m_grp) * MODES + mode - start
     source = jnp.where(mode < MODES, source, -1)
-    pick = jnp.where(iota((WINDOW, 40 * MEMBERS), 0) == source, 1.0, 0.0).astype(BF16)
+    pick = jnp.where(iota((WINDOW, 2 * WINDOW), 0) == source, 1.0, 0.0).astype(BF16)
     wait_recv(windows.at[0 : MEMBERS - 1], 1)
     high, low = split(windows[...].reshape(MEMBERS * 8, WINDOW))
     piece = mm(jnp.concatenate([high, low], axis=0), pick, NN).astype(BF16)
+    piece = jnp.concatenate([piece[:, :WINDOW], piece[:, WINDOW:]], axis=0)
 
     wait_recv(loads.at[0 : MEMBERS - 1], 2)
     every = loads[...]
     total = jnp.sum(every[:, 0:8, :], axis=0)
-    flat_load = every.reshape(MEMBERS * 40, 128)
-    high = flat_load.astype(BF16)
-    low = (flat_load - high.astype(F32)).astype(BF16)
-    both = jnp.where(iota((MEMBERS * 40, 128), 1) < 64, high.astype(F32), low.astype(F32)).astype(BF16)
-    part = mm(piece, both, NN)
-    part = part[:128] + part[128:]
+    total = jnp.where(left, total, pltpu.roll(total, 64, 1))
+    high, low = split(every.reshape(MEMBERS * 16, 128))
+    part = mm(piece, jnp.concatenate([high, low], axis=1), NN)
+    part = part[:, :128] + part[:, 128:]
+    part = jnp.where(
+        iota((128, 128), 1) < 64, part[:128] + part[128:256], part[256:384] + part[384:]
+    )
     part = part + pltpu.roll(part, 64, 1)
-    part = part.reshape(MEMBERS, 8, 128)
-    parts[...] = part + jnp.where(row >= 6, total, 0.0)[None]
+    part = part.reshape(MEMBERS, 8, 128) + jnp.where(row >= MODES, total, 0.0)[None]
+    parts[...] = jnp.where(left[None], part, pltpu.roll(part, 4, 1))[:, 0:4, :]
     for step in range(1, MEMBERS):
         other, target = peer(step)
         send(parts.at[other], got.at[block], 4, target)
     got[block] = parts[block]
     wait_recv(got.at[0 : MEMBERS - 1], 4)
     amp = jnp.sum(got[...], axis=0)
+    amp = jnp.concatenate([amp, pltpu.roll(amp, 64, 1)], axis=0)
+    amp = jnp.where(left, amp, pltpu.roll(amp, 64, 1))
     amps[0] = amp
     for f in range(4):
         send(amps.at[0], amps.at[1 + (f ^ 1)], 5, across[f])
@@ -298,12 +316,6 @@
     rr = column_of(amp[6:7, :])
     curvature = column_of(amp[7:8, :])
     step_size = rr / curvature
-    dirn = jnp.where(active, dir_v[...], 0.0)
-    copies_in["lam"].wait()
-    lam_v[...] = jnp.where(active, lam_v[...], 0.0) + step_size * dirn
-    lam_copy = pltpu.make_async_copy(lam_v, lam_out, out_sem.at[0])
-    lam_copy.start()
-
     wait_recv(nb_y, 3)
     wait_recv(amps.at[1:5], 5)
     spread = []
@@ -319,13 +331,13 @@
         image = own_y[f] + jnp.where(active_pad[:, cut], nb_y[f], 0.0)
         spread.append((image - back[:CASES])[:, :FACE])
     projected = jnp.concatenate(spread, axis=1)
+    proj_v[...] = projected
+    proj_copy = pltpu.make_async_copy(proj_v, proj_out, out_sem.at[0])
+    proj_copy.start()
     res = jnp.where(active, res_v[...], 0.0) - step_size * projected
-    res_v[...] = res
-    res_copy = pltpu.make_async_copy(res_v, res_out, out_sem.at[1])
-    res_copy.start()
 
     next_row = row_of(0.5 * jnp.sum(res * res, axis=1, keepdims=True))
-    norm_a[place] = jnp.broadcast_to(next_row, (8, 128))
+    norm_a[place] = next_row
     for step in range(1, MEMBERS):
         send(norm_a.at[place], norm_a.at[place], 6, mate(step))
     wait_recv(norm_a.at[0 : MEMBERS - 1], 6)
@@ -333,10 +345,8 @@
     for step in range(1, MEMBERS):
         send(norm_b.at[block], norm_b.at[block], 7, peer(step)[1])
     wait_recv(norm_b.at[0 : MEMBERS - 1], 7)
-    rr_next = column_of(jnp.sum(norm_b[...], axis=0)[0:1, :])
-    dir_v[...] = res + (rr_next / rr) * dirn
-    dir_copy = pltpu.make_async_copy(dir_v, dir_out, out_sem.at[2])
-    dir_copy.start()
+    rr_next = column_of(jnp.sum(norm_b[...], axis=0))
+    coef_out[...] = jnp.where(iota((CASES, 128), 1) < 64, step_size, rr_next / rr)
 
     wait_send(own_rf, 0)
     wait_send(windows.at[0 : MEMBERS - 1], 1)
@@ -346,9 +356,71 @@
     wait_send(amps.at[1:5], 5)
     wait_send(norm_a.at[0 : MEMBERS - 1], 6)
     wait_send(norm_b.at[0 : MEMBERS - 1], 7)
-    lam_copy.wait()
-    res_copy.wait()
-    dir_copy.wait()
+    proj_copy.wait()
+
+
+def update(
+    lam_hbm,
+    res_hbm,
+    dir_hbm,
+    proj_hbm,
+    coef_hbm,
+    sizes_hbm,
+    lam_out,
+    res_out,
+    dir_out,
+    proj_v,
+    coef_v,
+    sizes_ref,
+    lam_v,
+    res_v,
+    dir_v,
+    sem,
+):
+    ins = [
+        pltpu.make_async_copy(src, dst, sem.at[k])
+        for k, (src, dst) in enumerate(
+            (
+                (sizes_hbm, sizes_ref),
+                (dir_hbm, dir_v),
+                (lam_hbm, lam_v),
+                (coef_hbm, coef_v),
+                (res_hbm, res_v),
+                (proj_hbm, proj_v),
+            )
+        )
+    ]
+    for copy in ins:
+        copy.start()
+    outs = [
+        pltpu.make_async_copy(src, dst, sem.at[6 + k])
+        for k, (src, dst) in enumerate(((lam_v, lam_out), (res_v, res_out), (dir_v, dir_out)))
+    ]
+    ins[0].wait()
+    flat = iota((1, WIDTH), 1)
+    face = face_at(flat, FACE)
+    limit = jnp.zeros_like(face)
+    for f in range(4):
+        limit = jnp.where(face == f, sizes_ref[0, 0, f], limit)
+    active = (flat - face * FACE) < limit
+    ins[1].wait()
+    dirn = jnp.where(active, dir_v[...], 0.0)
+    ins[2].wait()
+    ins[3].wait()
+    coef = coef_v[...]
+    step_size = coef[:, 0:1]
+    ratio = coef[:, 64:65]
+    lam_v[...] = jnp.where(active, lam_v[...], 0.0) + step_size * dirn
+    outs[0].start()
+    ins[4].wait()
+    ins[5].wait()
+    res = jnp.where(active, res_v[...], 0.0) - step_size * proj_v[...]
+    res_v[...] = res
+    outs[1].start()
+    dir_v[...] = res + ratio * dirn
+    outs[2].start()
+    for copy in outs:
+        copy.wait()
 
 
 def on_device(
@@ -362,20 +434,25 @@
     slot_order,
 ):
     field = jax.ShapeDtypeStruct((CASES, WIDTH), F32)
-    anywhere = pl.BlockSpec(memory_space=pl.ANY)
-    outs = pl.pallas_call(
+    hbm = pl.BlockSpec(memory_space=pltpu.HBM)
+    vmem = pl.BlockSpec(memory_space=pltpu.VMEM)
+    projected, coef = pl.pallas_call(
         kernel,
-        out_shape=(field, field, field),
-        in_specs=[anywhere] * 6
-        + [pl.BlockSpec(memory_space=pltpu.SMEM), pl.BlockSpec(memory_space=pltpu.VMEM)],
-        out_specs=(anywhere, anywhere, anywhere),
+        out_shape=(
+            field,
+            jax.ShapeDtypeStruct((CASES, 128), F32),
+        ),
+        in_specs=[hbm] * 7,
+        out_specs=[hbm, vmem],
         scratch_shapes=[
             pltpu.VMEM((CASES, WIDTH), F32),
             pltpu.VMEM((CASES, WIDTH), F32),
             pltpu.VMEM((CASES, WIDTH), F32),
             pltpu.VMEM((WIDTH, WIDTH), F32),
-            pltpu.VMEM((MODES, WIDTH), F32),
+            pltpu.VMEM((MODES, 1, WIDTH), F32),
             pltpu.VMEM((MODES, COARSE), F32),
+            pltpu.VMEM((1, 1, WIDTH), jnp.int32),
+            pltpu.SMEM((1, 1, 4), jnp.int32),
             pltpu.VMEM((8, COARSE), F32),
             pltpu.VMEM((WIDE, WIDTH), BF16),
             pltpu.VMEM((4, 8, PAD), F32),
@@ -383,29 +460,51 @@
             pltpu.VMEM((4, CASES, PAD), F32),
             pltpu.VMEM((4, CASES, PAD), F32),
             pltpu.VMEM((MEMBERS, 8, WINDOW), F32),
-            pltpu.VMEM((MEMBERS, 40, 128), F32),
-            pltpu.VMEM((MEMBERS, 8, 128), F32),
-            pltpu.VMEM((MEMBERS, 8, 128), F32),
+            pltpu.VMEM((MEMBERS, 16, 128), F32),
+            pltpu.VMEM((MEMBERS, 4, 128), F32),
+            pltpu.VMEM((MEMBERS, 4, 128), F32),
             pltpu.VMEM((5, 8, 128), F32),
-            pltpu.VMEM((MEMBERS, 8, 128), F32),
-            pltpu.VMEM((MEMBERS, 8, 128), F32),
-            pltpu.SemaphoreType.DMA((6,)),
-            pltpu.SemaphoreType.DMA((3,)),
+            pltpu.VMEM((MEMBERS, 1, 128), F32),
+            pltpu.VMEM((MEMBERS, 1, 128), F32),
+            pltpu.SemaphoreType.DMA((7,)),
+            pltpu.SemaphoreType.DMA((1,)),
             pltpu.SemaphoreType.DMA((8,)),
             pltpu.SemaphoreType.DMA((8,)),
         ],
         compiler_params=pltpu.CompilerParams(
-            collective_id=0, has_side_effects=True, vmem_limit_bytes=48 * 1024 * 1024
+            collective_id=0, has_side_effects=True, vmem_limit_bytes=62 * 1024 * 1024
         ),
+    )(
+        residual.reshape(CASES, WIDTH),
+        direction.reshape(CASES, WIDTH),
+        dual_operator.reshape(WIDTH, WIDTH),
+        rigid_trace.transpose(0, 2, 1, 3).reshape(MODES, 1, WIDTH),
+        coarse_inverse,
+        face_sizes,
+        slot_order,
+    )
+    outs = pl.pallas_call(
+        update,
+        out_shape=(field, field, field),
+        in_specs=[hbm] * 6,
+        out_specs=[hbm, hbm, hbm],
+        scratch_shapes=[
+            pltpu.VMEM((CASES, WIDTH), F32),
+            pltpu.VMEM((CASES, 128), F32),
+            pltpu.SMEM((1, 1, 4), jnp.int32),
+            pltpu.VMEM((CASES, WIDTH), F32),
+            pltpu.VMEM((CASES, WIDTH), F32),
+            pltpu.VMEM((CASES, WIDTH), F32),
+            pltpu.SemaphoreType.DMA((9,)),
+        ],
+        compiler_params=pltpu.CompilerParams(vmem_limit_bytes=62 * 1024 * 1024),
     )(
         multipliers.reshape(CASES, WIDTH),
         residual.reshape(CASES, WIDTH),
         direction.reshape(CASES, WIDTH),
-        dual_operator.reshape(WIDTH, WIDTH),
-        rigid_trace.reshape(MODES, WIDTH),
-        coarse_inverse,
+        projected,
+        coef,
         face_sizes,
-        slot_order,
     )
     return tuple(x[None, None] for x in outs)
 

time: 53.8 us -> 42.6 us (0.79)
  local copies, waits for them, and re-layouts: 7.99 us -> 0 us
  Pallas kernels: 44.8 us -> 41.9 us
    unnamed x16 -> x0, local copies, waits for them, and re-layouts: 7.99 us -> none
    pallas_call x1 -> x2, Pallas kernels: 44.8 us -> 41.9 us  [the longest x1 39.6 us: on_device(): pl.pallas_call(kernel, out_shape=(field, jax.ShapeDtypeStruct((CASES, 128...]
where the time goes in v2:
time: 42.6 us; the launch traced here: 42.5 us
  Pallas kernels  41.9 us (98%)
  between operations  0.64 us (2%)
    pallas_call x1, Pallas kernels, on_device(): pl.pallas_call(kernel, out_shape=(field, jax.ShapeDtypeStruct((CASES, 128...  39.6 us
    pallas_call x1, Pallas kernels, on_device(): pl.pallas_call(update, out_shape=(field, field, field), in_specs=[hbm] *...  2.24 us

profile of v2, /device:TPU:1, one launch (start us, length us, event | category | flops | bytes accessed | tf_op | source)
XLA Modules:
  0.0 42.5 jit_solution(11262647293226863891)
XLA Ops:
  0.6 39.6 %shard_map.103 = (f32[64,1200]{1,0:T(8,128)}, f32[64,128]{1,0:T(8,128)}) custom-call(f32[64,1200]{1,0:T(8,128)} %bitcast.9, f32[64,1200]{1,0:T(8,128)} %bitcast.11, f32[1200,1200]{1,0:T(8,128)} %bitcast.8, f32[6,1,1200]{2,1,0:T(1,128)} %bitcast.14, f32[6,1536]{1,0:T(8,128)} %inv_hbm.1, s32[1,1,4]{2,1,0:T(1,128)} %sizes_hbm.3, s32[1,1,1200]{2,1,0:T(1,128)} %order_hbm.1), custom_call_target="tpu_custom_call" | custom-call | tf_op jit(solution)/shard_map/pallas_call | solution.py:439
  40.3 2.2 %shard_map.104 = (f32[64,1200]{1,0:T(8,128)}, f32[64,1200]{1,0:T(8,128)}, f32[64,1200]{1,0:T(8,128)}) custom-call(f32[64,1200]{1,0:T(8,128)} %bitcast.13, f32[64,1200]{1,0:T(8,128)} %bitcast.10, f32[64,1200]{1,0:T(8,128)} %bitcast.12, f32[64,1200]{1,0:T(8,128)} %get-tuple-element.8.proj_hbm, f32[64,128]{1,0:T(8,128)} %get-tuple-element.9.coef_hbm, ...), custom_call_target="tpu_custom_call" | custom-call | tf_op jit(solution)/shard_map/pallas_call | solution.py:486

commit v3 on v2

v3 whole, which is shorter than its diff:
```python
import functools

import jax
import jax.numpy as jnp
from jax import lax
from jax.experimental import pallas as pl
from jax.experimental.pallas import tpu as pltpu
from jax.sharding import PartitionSpec as P

MESH = pl.DeviceIdType.MESH
F32 = jnp.float32
BF16 = jnp.bfloat16
NN = (((1,), (0,)), ((), ()))
NT = (((1,), (1,)), ((), ()))
TN = (((0,), (0,)), ((), ()))

CASES = 64
WIDTH = 1200
FACE = 300
PAD = 384
WIDE = 4 * PAD
MODES = 6
COARSE = 1536
PAIRS = 32
MATES = 8


def split(x):
    high = x.astype(BF16)
    return high, (x - high.astype(F32)).astype(BF16)


def mm(a, b, dims):
    return lax.dot_general(a, b, dims, preferred_element_type=F32)


def iota(shape, dim):
    return lax.broadcasted_iota(jnp.int32, shape, dim)


def face_at(lane, step):
    one = jnp.int32(1)
    zero = jnp.int32(0)
    return (
        jnp.where(lane >= step, one, zero)
        + jnp.where(lane >= 2 * step, one, zero)
        + jnp.where(lane >= 3 * step, one, zero)
    )


def row_of(column):
    eye = iota((CASES, 128), 0) == iota((CASES, 128), 1)
    return jnp.sum(jnp.where(eye, column, 0.0), axis=0, keepdims=True)


def column_of(row):
    eye = iota((CASES, 128), 0) == iota((CASES, 128), 1)
    return jnp.sum(jnp.where(eye, row, 0.0), axis=1, keepdims=True)


def packed(tile):
    left = iota((8, 128), 1) < 64
    return jnp.where(left, tile, pltpu.roll(tile, 4, 0))[0:4]


def unpacked(half):
    return jnp.concatenate([half, pltpu.roll(half, 64, half.ndim - 1)], axis=half.ndim - 2)


def doubled(x):
    return jnp.where(iota(x.shape, 1) < 64, x, pltpu.roll(x, 64, 1))


def lanes_split(x):
    high = x.astype(BF16).astype(F32)
    return jnp.where(iota(x.shape, 1) < 64, high, x - high).astype(BF16)


def both_sides(x):
    other = pltpu.roll(x, 64, 1)
    left = iota(x.shape, 1) < 64
    return jnp.concatenate(
        [lanes_split(jnp.where(left, x, other)), lanes_split(jnp.where(left, other, x))], axis=0
    )


def summed(x):
    return x + pltpu.roll(x, 64, 1)


def kernel(
    res_hbm,
    dir_hbm,
    dual_hbm,
    trace_hbm,
    inv_hbm,
    sizes_hbm,
    order_hbm,
    res_out,
    coef_out,
    next_v,
    res_v,
    dir_v,
    dual_v,
    trace_v,
    inv_v,
    order_ref,
    sizes_ref,
    perm,
    halves,
    own_rf,
    nb_rf,
    res_pad,
    own_y,
    nb_y,
    rows_out,
    rows_in,
    loads,
    parts,
    got,
    grams,
    amps,
    norms,
    in_sem,
    out_sem,
    send_sem,
    recv_sem,
):
    s = lax.axis_index("sub")
    g = lax.axis_index("grp")
    pair = s // 2
    core = s % 2
    place = core * 4 + g

    copies_in = {}
    for k, (name, src, dst) in enumerate(
        (
            ("sizes", sizes_hbm, sizes_ref),
            ("order", order_hbm, order_ref),
            ("trace", trace_hbm, trace_v),
            ("dir", dir_hbm, dir_v),
            ("inv", inv_hbm, inv_v),
            ("dual", dual_hbm, dual_v),
            ("res", res_hbm, res_v),
        )
    ):
        copies_in[name] = pltpu.make_async_copy(src, dst, in_sem.at[k])
        copies_in[name].start()

    across = (
        ((s + 63) % 64, g),
        ((s + 1) % 64, g),
        (s, (g + 3) % 4),
        (s, (g + 1) % 4),
    )

    def mate(step):
        other = (place + step) % MATES
        return (pair * 2 + other // 4, other % 4)

    def peer(step):
        other = (pair + step) % PAIRS
        return other, (other * 2 + core, g)

    beside = (pair + 2 * core - 1 + PAIRS) % PAIRS

    barrier = pltpu.get_barrier_semaphore()
    for step in range(1, PAIRS):
        pl.semaphore_signal(barrier, inc=1, device_id=peer(step)[1], device_id_type=MESH)
    for other in range(4):
        for target in ((2 * pair + 63) % 64, other), ((2 * pair + 2) % 64, other):
            pl.semaphore_signal(barrier, inc=1, device_id=target, device_id_type=MESH)
    for step in range(1, MATES):
        pl.semaphore_signal(barrier, inc=1, device_id=mate(step), device_id_type=MESH)

    def send(src, dst, phase, target):
        pltpu.make_async_remote_copy(
            src_ref=src,
            dst_ref=dst,
            send_sem=send_sem.at[phase],
            recv_sem=recv_sem.at[phase],
            device_id=target,
            device_id_type=MESH,
        ).start()

    def wait_recv(ref, phase):
        pltpu.make_async_copy(ref, ref, recv_sem.at[phase]).wait()

    def wait_send(ref, phase):
        pltpu.make_async_copy(ref, ref, send_sem.at[phase]).wait()

    def greeted():
        pl.semaphore_wait(barrier, PAIRS - 1 + 8 + MATES - 1)
        for f in range(4):
            send(own_rf.at[f], nb_rf.at[f ^ 1], 0, across[f])
        for step in range(1, PAIRS):
            other, target = peer(step)
            send(rows_out.at[other], rows_in.at[pair], 1, target)

    copies_in["sizes"].wait()
    copies_in["order"].wait()

    def limits(face):
        out = jnp.zeros_like(face)
        for f in range(4):
            out = jnp.where(face == f, sizes_ref[0, 0, f], out)
        return out

    lane = iota((1, WIDE), 1)
    face = face_at(lane, PAD)
    active_pad = (lane - face * PAD) < limits(face)
    sign_pad = jnp.where((face & 1) == 0, -1.0, 1.0)
    mask_pad = jnp.where(active_pad, sign_pad, 0.0)
    left = iota((8, 128), 1) < 64
    row = iota((8, 128), 0)

    order = order_ref[0]
    order = order + (PAD - FACE) * face_at(order, FACE)
    line = lax.broadcasted_iota(jnp.int16, (PAD, WIDTH), 0)
    ones = jnp.ones((PAD, WIDTH), BF16)
    for f in range(4):
        hot = line == jnp.broadcast_to((order - f * PAD).astype(jnp.int16), (PAD, WIDTH))
        perm[f * PAD : (f + 1) * PAD, :] = jnp.where(hot, ones, jnp.zeros_like(ones))

    copies_in["trace"].wait()
    trace = jnp.concatenate([trace_v[...].reshape(MODES, WIDTH), jnp.zeros((2, WIDTH), F32)], axis=0)
    high, low = split(trace)
    both = jnp.concatenate([high.astype(F32), low.astype(F32)], axis=0).astype(BF16)
    for f in range(4):
        got_rf = mm(both, perm[f * PAD : (f + 1) * PAD, :], NT)
        own_rf[f] = (got_rf[:8] + got_rf[8:]) * mask_pad[:, f * PAD : (f + 1) * PAD]

    copies_in["inv"].wait()
    rows = jnp.concatenate([inv_v[...], jnp.zeros((2, COARSE), F32)], axis=0)
    rows = jnp.concatenate([jnp.zeros((8, 24), F32), rows, jnp.zeros((8, 104), F32)], axis=1)
    for p in range(PAIRS):
        rows_out[p] = rows[:, 48 * p : 48 * p + 128]

    def padded(x):
        gap = jnp.zeros((CASES, PAD - FACE), F32)
        spread = []
        for f in range(4):
            spread += [x[:, f * FACE : (f + 1) * FACE], gap]
        return jnp.where(active_pad, jnp.concatenate(spread, axis=1), 0.0)

    copies_in["dir"].wait()
    dir_pad = padded(dir_v[...])
    dir_high, dir_low = split(dir_pad * sign_pad)
    slots = mm(jnp.concatenate([dir_high, dir_low], axis=0), perm[...], NN)
    slots = slots[:CASES] + slots[CASES:]

    high, low = split(slots)
    both = jnp.concatenate([high, low], axis=0)
    copies_in["dual"].wait()
    for k in range(0, WIDTH, 240):
        if k == 480:
            greeted()
        f_high, f_low = split(dual_v[k : k + 240, :])
        z_high, z_low = split(mm(f_high, both, NT) + mm(f_low, both, NT))
        halves[k : k + 240, 0:128] = z_high
        halves[k : k + 240, 128:256] = z_low

    ys = []
    for f in range(4):
        y = mm(perm[f * PAD : (f + 1) * PAD, :], halves[...], NN)
        ys.append(y[:, :128] + y[:, 128:])
    copies_in["res"].wait()
    flat = iota((1, WIDTH), 1)
    flat_face = face_at(flat, FACE)
    active = (flat - flat_face * FACE) < limits(flat_face)
    res = jnp.where(active, res_v[...], 0.0)
    rr_row = row_of(0.5 * jnp.sum(res * res, axis=1, keepdims=True))
    wait_recv(nb_rf, 0)
    own_load = jnp.zeros((8, 128), F32)
    curvature = jnp.zeros((CASES, 128), F32)
    nb_load = []
    for f in range(4):
        cut = slice(f * PAD, (f + 1) * PAD)
        nb_rf[f] = jnp.where(active_pad[:, cut], nb_rf[f], 0.0)
        r_high, r_low = split(jnp.concatenate([own_rf[f], nb_rf[f]], axis=0))
        y_high, y_low = split(ys[f])
        piece = mm(
            jnp.concatenate([r_high, r_low, dir_high[:, cut], dir_low[:, cut]], axis=0),
            jnp.concatenate([y_high, y_low], axis=1),
            NN,
        )
        piece = piece[:, :128] + piece[:, 128:]
        curvature = curvature + piece[32 : 32 + CASES] + piece[32 + CASES :]
        piece = piece[:16] + piece[16:32]
        if not f & 1:
            piece = -piece
        own_load = own_load + piece[:8]
        nb_load.append(summed(piece[8:]))
    own_load = summed(own_load)
    diagonal = (iota((CASES, 128), 1) & 63) == iota((CASES, 128), 0)
    curv_row = summed(jnp.sum(jnp.where(diagonal, curvature, 0.0), axis=0, keepdims=True))
    own_load = jnp.where(row == 6, rr_row, jnp.where(row == 7, curv_row, own_load))
    for f in range(3):
        moved = pltpu.roll(nb_load[3], 6 - 2 * f, 0)
        nb_load[f] = jnp.where(row < MODES, nb_load[f], moved)
    loads[place, 0:8, :] = jnp.where(left, own_load, nb_load[0])
    loads[place, 8:16, :] = jnp.where(left, nb_load[1], nb_load[2])
    for step in range(1, MATES):
        send(loads.at[place], loads.at[place], 2, mate(step))
    for f in range(4):
        y = jnp.transpose(ys[f])
        y = (y[:CASES] + y[CASES:]) * mask_pad[:, f * PAD : (f + 1) * PAD]
        own_y[f] = y
        send(own_y.at[f], nb_y.at[f ^ 1], 3, across[f])
    res = padded(res)
    for f in range(4):
        res_pad[f] = res[:, f * PAD : (f + 1) * PAD]

    col = iota((1, 256), 1)
    mode = col & 7
    tile = 2 * ((col >> 3) & 1) + (col >> 7)
    member = (col >> 4) & 7
    spare = (mode >= MODES) & (tile > 0)
    group = jnp.where(spare, 4, tile)
    mode = jnp.where(spare, 2 * (tile - 1) + mode - MODES, mode)
    d_sub = jnp.where(group == 1, -1, jnp.where(group == 2, 1, 0))
    d_grp = jnp.where(group == 3, -1, jnp.where(group == 4, 1, 0))
    source = ((member >> 2) + d_sub + 1) * 24 + ((member & 3) + d_grp) * MODES + mode
    source = jnp.where(mode < MODES, source, -1)
    pick = jnp.where(iota((128, 256), 0) == source, 1.0, 0.0).astype(BF16)

    slots_of = (
        place,
        core * g + (1 - core) * (8 + g),
        core * (12 + g) + (1 - core) * (4 + g),
        core * 4 + (g + 3) % 4,
        core * 4 + (g + 1) % 4,
    )
    lane = iota((32, 128), 1)
    line = iota((32, 128), 0)
    mode = 4 * (lane >> 6) + (lane & 3)
    slot = (lane >> 2) & 15
    gram = jnp.zeros((8, 128), F32)
    for f in range(4):
        r_high, r_low = split(own_rf[f])
        n_high, n_low = split(jnp.concatenate([own_rf[f], nb_rf[f]], axis=0))
        piece = mm(
            jnp.concatenate([r_high, r_low], axis=0), jnp.concatenate([n_high, n_low], axis=0), NT
        )
        piece_high, piece_low = split(piece[:8] + piece[8:])
        wanted = jnp.where((line & 8) == 0, slots_of[0], slots_of[1 + f])
        hot = ((line & 7) == mode) & (mode < MODES) & (slot == wanted)
        piece = mm(
            jnp.concatenate([piece_high, piece_low], axis=0),
            jnp.where(hot, 1.0, 0.0).astype(BF16),
            NN,
        )
        gram = gram + piece[:8] + piece[8:]
    grams[place] = gram
    for step in range(1, MATES):
        send(grams.at[place], grams.at[place], 4, mate(step))

    rows_in[pair] = rows_out[pair]
    wait_recv(rows_in.at[0 : PAIRS - 1], 1)
    high, low = split(rows_in[...].reshape(PAIRS * 8, 128))
    piece = mm(jnp.concatenate([high, low], axis=0), pick, NN).astype(BF16)
    piece = jnp.concatenate([piece[: PAIRS * 8], piece[PAIRS * 8 :]], axis=1)

    wait_recv(loads.at[0 : MATES - 1], 2)
    every = loads[...]
    total = doubled(jnp.sum(every[:, 0:8, :], axis=0))
    line = both_sides(every.reshape(MATES * 16, 128))
    part = summed(mm(piece, jnp.concatenate([line, line], axis=0), NN))
    part = part.reshape(PAIRS, 8, 128) + jnp.where(row >= MODES, total, 0.0)[None]
    parts[...] = jnp.where(left[None], part, pltpu.roll(part, 4, 1))[:, 0:4, :]
    for step in range(1, PAIRS):
        other, target = peer(step)
        send(parts.at[other], got.at[pair], 5, target)
    got[pair] = parts[pair]

    wait_recv(nb_y, 3)
    trace_res = jnp.zeros((8, 128), F32)
    trace_image = jnp.zeros((8, 128), F32)
    for f in range(4):
        image = own_y[f] + jnp.where(active_pad[:, f * PAD : (f + 1) * PAD], nb_y[f], 0.0)
        nb_y[f] = image
        r_high, r_low = split(own_rf[f])
        b_high, b_low = split(jnp.concatenate([res_pad[f], image], axis=0))
        piece = mm(
            jnp.concatenate([r_high, r_low], axis=0),
            jnp.concatenate(
                [b_high[:CASES], b_low[:CASES], b_high[CASES:], b_low[CASES:]], axis=0
            ),
            NT,
        )
        piece = piece[:8] + piece[8:]
        trace_res = trace_res + piece[:, :128]
        trace_image = trace_image + piece[:, 128:]
    trace_res = summed(trace_res)
    trace_image = summed(trace_image)
    wait_recv(grams.at[0 : MATES - 1], 4)
    high, low = split(grams[...].reshape(MATES * 8, 128))
    gram = jnp.concatenate([high, low], axis=1)

    wait_recv(got.at[0 : PAIRS - 1], 5)
    amp = doubled(unpacked(jnp.sum(got[...], axis=0)))
    rr_row = amp[6:7, :]
    step_row = rr_row / amp[7:8, :]
    step_size = column_of(step_row)
    square = jnp.zeros((CASES, 128), F32)
    for f in range(4):
        u = res_pad[f] - step_size * nb_y[f]
        res_pad[f] = u
        for k in range(0, PAD, 128):
            square = square + u[:, k : k + 128] * u[:, k : k + 128]
    u_row = row_of(0.5 * jnp.sum(square, axis=1, keepdims=True))
    scaled = jnp.where(row < MODES, step_row * amp, 0.0)
    cross = jnp.sum(scaled * (trace_res - step_row * trace_image), axis=0, keepdims=True)
    own = jnp.where(row == 6, doubled(u_row + 2.0 * cross), scaled)
    amps[place] = packed(own)
    slot = 12 - 4 * core + g
    for other in range(8):
        send(amps.at[place], amps.at[slot], 6, (2 * beside + other // 4, other % 4))
    for step in range(1, MATES):
        send(amps.at[place], amps.at[place], 6, mate(step))
    wait_recv(amps.at[0:15], 6)
    every = amps[...]
    line = both_sides(every.reshape(64, 128))
    image = summed(mm(gram, jnp.concatenate([line, line], axis=0), NN))
    mates = unpacked(every[0:MATES]).reshape(MATES * 8, 128)
    spare = (iota((MATES * 8, 128), 0) & 7) >= MODES
    norm = jnp.sum(jnp.where(spare, mates, mates * image), axis=0, keepdims=True)
    norms[pair] = norm
    for step in range(1, PAIRS):
        send(norms.at[pair], norms.at[pair], 7, peer(step)[1])

    spread = []
    for f in range(4):
        a_high, a_low = split(jnp.concatenate([own, unpacked(amps[slots_of[1 + f]])], axis=0))
        r_high, r_low = split(jnp.concatenate([own_rf[f], nb_rf[f]], axis=0))
        back = mm(
            jnp.concatenate([a_high, a_low, a_high, a_low], axis=0),
            jnp.concatenate([r_high, r_high, r_low, r_low], axis=0),
            TN,
        )
        spread.append((res_pad[f] + back[:CASES])[:, :FACE])
    next_v[...] = jnp.concatenate(spread, axis=1)
    next_copy = pltpu.make_async_copy(next_v, res_out, out_sem.at[0])
    next_copy.start()
    wait_recv(norms.at[0 : PAIRS - 1], 7)
    ratio = column_of(jnp.sum(norms[...], axis=0) / rr_row)
    coef_out[...] = jnp.where(iota((CASES, 128), 1) < 64, step_size, ratio)

    wait_send(own_rf, 0)
    wait_send(rows_in.at[0 : PAIRS - 1], 1)
    wait_send(loads.at[0 : MATES - 1], 2)
    wait_send(own_y, 3)
    wait_send(grams.at[0 : MATES - 1], 4)
    wait_send(parts.at[0 : PAIRS - 1], 5)
    wait_send(amps.at[0:15], 6)
    wait_send(norms.at[0 : PAIRS - 1], 7)
    next_copy.wait()


def update(
    lam_hbm,
    dir_hbm,
    res_hbm,
    coef_hbm,
    sizes_hbm,
    lam_out,
    res_out,
    dir_out,
    coef_v,
    sizes_ref,
    lam_v,
    res_v,
    dir_v,
    sem,
):
    ins = [
        pltpu.make_async_copy(src, dst, sem.at[k])
        for k, (src, dst) in enumerate(
            (
                (sizes_hbm, sizes_ref),
                (dir_hbm, dir_v),
                (lam_hbm, lam_v),
                (coef_hbm, coef_v),
                (res_hbm, res_v),
            )
        )
    ]
    for copy in ins:
        copy.start()
    outs = [
        pltpu.make_async_copy(src, dst, sem.at[5 + k])
        for k, (src, dst) in enumerate(((lam_v, lam_out), (res_v, res_out), (dir_v, dir_out)))
    ]
    ins[0].wait()
    flat = iota((1, WIDTH), 1)
    face = face_at(flat, FACE)
    limit = jnp.zeros_like(face)
    for f in range(4):
        limit = jnp.where(face == f, sizes_ref[0, 0, f], limit)
    active = (flat - face * FACE) < limit
    ins[1].wait()
    dirn = jnp.where(active, dir_v[...], 0.0)
    ins[2].wait()
    ins[3].wait()
    coef = coef_v[...]
    step_size = coef[:, 0:1]
    ratio = coef[:, 64:65]
    lam_v[...] = jnp.where(active, lam_v[...], 0.0) + step_size * dirn
    outs[0].start()
    ins[4].wait()
    outs[1].start()
    dir_v[...] = res_v[...] + ratio * dirn
    outs[2].start()
    for copy in outs:
        copy.wait()


def on_device(
    multipliers,
    residual,
    direction,
    dual_operator,
    rigid_trace,
    coarse_inverse,
    face_sizes,
    slot_order,
):
    field = jax.ShapeDtypeStruct((CASES, WIDTH), F32)
    hbm = pl.BlockSpec(memory_space=pltpu.HBM)
    vmem = pl.BlockSpec(memory_space=pltpu.VMEM)
    res_next, coef = pl.pallas_call(
        kernel,
        out_shape=(field, jax.ShapeDtypeStruct((CASES, 128), F32)),
        in_specs=[hbm] * 7,
        out_specs=[hbm, vmem],
        scratch_shapes=[
            pltpu.VMEM((CASES, WIDTH), F32),
            pltpu.VMEM((CASES, WIDTH), F32),
            pltpu.VMEM((CASES, WIDTH), F32),
            pltpu.VMEM((WIDTH, WIDTH), F32),
            pltpu.VMEM((MODES, 1, WIDTH), F32),
            pltpu.VMEM((MODES, COARSE), F32),
            pltpu.VMEM((1, 1, WIDTH), jnp.int32),
            pltpu.SMEM((1, 1, 4), jnp.int32),
            pltpu.VMEM((WIDE, WIDTH), BF16),
            pltpu.VMEM((WIDTH, 256), BF16),
            pltpu.VMEM((4, 8, PAD), F32),
            pltpu.VMEM((4, 8, PAD), F32),
            pltpu.VMEM((4, CASES, PAD), F32),
            pltpu.VMEM((4, CASES, PAD), F32),
            pltpu.VMEM((4, CASES, PAD), F32),
            pltpu.VMEM((PAIRS, 8, 128), F32),
            pltpu.VMEM((PAIRS, 8, 128), F32),
            pltpu.VMEM((MATES, 16, 128), F32),
            pltpu.VMEM((PAIRS, 4, 128), F32),
            pltpu.VMEM((PAIRS, 4, 128), F32),
            pltpu.VMEM((MATES, 8, 128), F32),
            pltpu.VMEM((16, 4, 128), F32),
            pltpu.VMEM((PAIRS, 1, 128), F32),
            pltpu.SemaphoreType.DMA((7,)),
            pltpu.SemaphoreType.DMA((1,)),
            pltpu.SemaphoreType.DMA((8,)),
            pltpu.SemaphoreType.DMA((8,)),
        ],
        compiler_params=pltpu.CompilerParams(
            collective_id=0, has_side_effects=True, vmem_limit_bytes=62 * 1024 * 1024
        ),
    )(
        residual.reshape(CASES, WIDTH),
        direction.reshape(CASES, WIDTH),
        dual_operator.reshape(WIDTH, WIDTH),
        rigid_trace.transpose(0, 2, 1, 3).reshape(MODES, 1, WIDTH),
        coarse_inverse,
        face_sizes,
        slot_order,
    )
    outs = pl.pallas_call(
        update,
        out_shape=(field, field, field),
        in_specs=[hbm] * 5,
        out_specs=[hbm, hbm, hbm],
        scratch_shapes=[
            pltpu.VMEM((CASES, 128), F32),
            pltpu.SMEM((1, 1, 4), jnp.int32),
            pltpu.VMEM((CASES, WIDTH), F32),
            pltpu.VMEM((CASES, WIDTH), F32),
            pltpu.VMEM((CASES, WIDTH), F32),
            pltpu.SemaphoreType.DMA((8,)),
        ],
        compiler_params=pltpu.CompilerParams(vmem_limit_bytes=62 * 1024 * 1024),
    )(
        multipliers.reshape(CASES, WIDTH),
        direction.reshape(CASES, WIDTH),
        res_next,
        coef,
        face_sizes,
    )
    return tuple(x[None, None] for x in outs)


def solution(mesh):
    wide = P("sub", "grp", None, None)
    return jax.shard_map(
        on_device,
        mesh=mesh,
        in_specs=(wide, wide, wide, wide, wide, P(("sub", "grp"), None), P("sub", "grp", None), P("sub", "grp", None)),
        out_specs=(wide, wide, wide),
        check_vma=False,
    )
```

time: 42.6 us -> 39.6 us (0.930)
  Pallas kernels: 41.9 us -> 38.8 us
    pallas_call x1, Pallas kernels: 39.6 us -> 36.7 us  [on_device(): pl.pallas_call(kernel, out_shape=(field, jax.ShapeDtypeStruct((CASES, 128...]
where the time goes in v3:
time: 39.6 us; the launch traced here: 39.5 us
  Pallas kernels  38.8 us (98%)
  between operations  0.64 us (2%)
    pallas_call x1, Pallas kernels, on_device(): pl.pallas_call(kernel, out_shape=(field, jax.ShapeDtypeStruct((CASES, 128...  36.7 us
    pallas_call x1, Pallas kernels, on_device(): pl.pallas_call(update, out_shape=(field, field, field), in_specs=[hbm] *...  2.19 us

profile of v3, /device:TPU:1, one launch (start us, length us, event | category | flops | bytes accessed | tf_op | source)
XLA Modules:
  0.0 39.5 jit_solution(822940673477373044)
XLA Ops:
  0.6 36.7 %shard_map.103 = (f32[64,1200]{1,0:T(8,128)}, f32[64,128]{1,0:T(8,128)}) custom-call(f32[64,1200]{1,0:T(8,128)} %bitcast.11, f32[64,1200]{1,0:T(8,128)} %bitcast.9, f32[1200,1200]{1,0:T(8,128)} %bitcast.8, f32[6,1,1200]{2,1,0:T(1,128)} %bitcast.13, f32[6,1536]{1,0:T(8,128)} %inv_hbm.1, s32[1,1,4]{2,1,0:T(1,128)} %sizes_hbm.3, s32[1,1,1200]{2,1,0:T(1,128)} %order_hbm.1), custom_call_target="tpu_custom_call" | custom-call | tf_op jit(solution)/shard_map/pallas_call | solution.py:531
  37.3 2.2 %shard_map.104 = (f32[64,1200]{1,0:T(8,128)}, f32[64,1200]{1,0:T(8,128)}, f32[64,1200]{1,0:T(8,128)}) custom-call(f32[64,1200]{1,0:T(8,128)} %bitcast.12, f32[64,1200]{1,0:T(8,128)} %bitcast.10, f32[64,1200]{1,0:T(8,128)} %get-tuple-element.8.res_hbm, f32[64,128]{1,0:T(8,128)} %get-tuple-element.9.coef_hbm, s32[1,1,4]{2,1,0:T(1,128)} %sizes_hbm.3), custom_call_target="tpu_custom_call" | custom-call | tf_op jit(solution)/shard_map/pallas_call | solution.py:577

commit v4 on v3

--- a/solution.py
+++ b/solution.py
@@ -18,11 +18,17 @@
 WIDTH = 1200
 FACE = 300
 PAD = 384
+ROWS = 304
 WIDE = 4 * PAD
 MODES = 6
 COARSE = 1536
 PAIRS = 32
 MATES = 8
+BARRIER_AT = 240
+PEERS = sorted(
+    ((dx, dz) for dx in range(4) for dz in range(8) if dx or dz),
+    key=lambda step: -min(step[0], 4 - step[0]) - min(step[1], 8 - step[1]),
+)
 
 
 def split(x):
@@ -99,6 +105,7 @@
     res_out,
     coef_out,
     next_v,
+    coef_v,
     res_v,
     dir_v,
     dual_v,
@@ -147,6 +154,7 @@
         copies_in[name] = pltpu.make_async_copy(src, dst, in_sem.at[k])
         copies_in[name].start()
 
+    rows_in[...] = jnp.zeros_like(rows_in)
     across = (
         ((s + 63) % 64, g),
         ((s + 1) % 64, g),
@@ -159,13 +167,14 @@
         return (pair * 2 + other // 4, other % 4)
 
     def peer(step):
-        other = (pair + step) % PAIRS
+        dx, dz = step
+        other = (pair // 8 + dx) % 4 * 8 + (pair + dz) % 8
         return other, (other * 2 + core, g)
 
     beside = (pair + 2 * core - 1 + PAIRS) % PAIRS
 
     barrier = pltpu.get_barrier_semaphore()
-    for step in range(1, PAIRS):
+    for step in PEERS:
         pl.semaphore_signal(barrier, inc=1, device_id=peer(step)[1], device_id_type=MESH)
     for other in range(4):
         for target in ((2 * pair + 63) % 64, other), ((2 * pair + 2) % 64, other):
@@ -193,9 +202,9 @@
         pl.semaphore_wait(barrier, PAIRS - 1 + 8 + MATES - 1)
         for f in range(4):
             send(own_rf.at[f], nb_rf.at[f ^ 1], 0, across[f])
-        for step in range(1, PAIRS):
+        for step in PEERS:
             other, target = peer(step)
-            send(rows_out.at[other], rows_in.at[pair], 1, target)
+            send(rows_out.at[other, 0:MODES], rows_in.at[pair, 0:MODES], 1, target)
 
     copies_in["sizes"].wait()
     copies_in["order"].wait()
@@ -211,24 +220,29 @@
     active_pad = (lane - face * PAD) < limits(face)
     sign_pad = jnp.where((face & 1) == 0, -1.0, 1.0)
     mask_pad = jnp.where(active_pad, sign_pad, 0.0)
+    lane = iota((1, 4 * ROWS), 1)
+    face = face_at(lane, ROWS)
+    active_row = (lane - face * ROWS) < limits(face)
+    mask_row = jnp.where(active_row, jnp.where((face & 1) == 0, -1.0, 1.0), 0.0)
     left = iota((8, 128), 1) < 64
     row = iota((8, 128), 0)
 
     order = order_ref[0]
-    order = order + (PAD - FACE) * face_at(order, FACE)
-    line = lax.broadcasted_iota(jnp.int16, (PAD, WIDTH), 0)
-    ones = jnp.ones((PAD, WIDTH), BF16)
-    for f in range(4):
-        hot = line == jnp.broadcast_to((order - f * PAD).astype(jnp.int16), (PAD, WIDTH))
-        perm[f * PAD : (f + 1) * PAD, :] = jnp.where(hot, ones, jnp.zeros_like(ones))
+    order = order + (ROWS - FACE) * face_at(order, FACE)
+    line = lax.broadcasted_iota(jnp.int16, (ROWS, WIDTH), 0)
+    ones = jnp.ones((ROWS, WIDTH), BF16)
+    for f in range(4):
+        hot = line == jnp.broadcast_to((order - f * ROWS).astype(jnp.int16), (ROWS, WIDTH))
+        perm[f * ROWS : (f + 1) * ROWS, :] = jnp.where(hot, ones, jnp.zeros_like(ones))
 
     copies_in["trace"].wait()
     trace = jnp.concatenate([trace_v[...].reshape(MODES, WIDTH), jnp.zeros((2, WIDTH), F32)], axis=0)
-    high, low = split(trace)
-    both = jnp.concatenate([high.astype(F32), low.astype(F32)], axis=0).astype(BF16)
-    for f in range(4):
-        got_rf = mm(both, perm[f * PAD : (f + 1) * PAD, :], NT)
-        own_rf[f] = (got_rf[:8] + got_rf[8:]) * mask_pad[:, f * PAD : (f + 1) * PAD]
+    low = trace - trace.astype(BF16).astype(F32)
+    got_rf = mm(jnp.concatenate([trace, low], axis=0).astype(BF16), perm[...], NT)
+    got_rf = (got_rf[:8] + got_rf[8:]) * mask_row
+    for f in range(4):
+        cut = got_rf[:, f * ROWS : (f + 1) * ROWS]
+        own_rf[f] = jnp.concatenate([cut, jnp.zeros((8, PAD - ROWS), F32)], axis=1)
 
     copies_in["inv"].wait()
     rows = jnp.concatenate([inv_v[...], jnp.zeros((2, COARSE), F32)], axis=0)
@@ -236,24 +250,23 @@
     for p in range(PAIRS):
         rows_out[p] = rows[:, 48 * p : 48 * p + 128]
 
-    def padded(x):
-        gap = jnp.zeros((CASES, PAD - FACE), F32)
+    def padded(x, width):
+        gap = jnp.zeros((CASES, width - FACE), F32)
         spread = []
         for f in range(4):
             spread += [x[:, f * FACE : (f + 1) * FACE], gap]
-        return jnp.where(active_pad, jnp.concatenate(spread, axis=1), 0.0)
+        return jnp.concatenate(spread, axis=1)
 
     copies_in["dir"].wait()
-    dir_pad = padded(dir_v[...])
-    dir_high, dir_low = split(dir_pad * sign_pad)
-    slots = mm(jnp.concatenate([dir_high, dir_low], axis=0), perm[...], NN)
+    high, low = split(padded(dir_v[...], ROWS) * mask_row)
+    slots = mm(jnp.concatenate([high, low], axis=0), perm[...], NN)
     slots = slots[:CASES] + slots[CASES:]
 
     high, low = split(slots)
     both = jnp.concatenate([high, low], axis=0)
     copies_in["dual"].wait()
     for k in range(0, WIDTH, 240):
-        if k == 480:
+        if k == BARRIER_AT:
             greeted()
         f_high, f_low = split(dual_v[k : k + 240, :])
         z_high, z_low = split(mm(f_high, both, NT) + mm(f_low, both, NT))
@@ -262,8 +275,13 @@
 
     ys = []
     for f in range(4):
-        y = mm(perm[f * PAD : (f + 1) * PAD, :], halves[...], NN)
+        y = mm(perm[f * ROWS : (f + 1) * ROWS, :], halves[...], NN)
         ys.append(y[:, :128] + y[:, 128:])
+    curvature = mm(both, halves[...], NN)
+    curvature = curvature[:, :128] + curvature[:, 128:]
+    curvature = curvature[:CASES] + curvature[CASES:]
+    diagonal = (iota((CASES, 128), 1) & 63) == iota((CASES, 128), 0)
+    curv_row = summed(jnp.sum(jnp.where(diagonal, curvature, 0.0), axis=0, keepdims=True))
     copies_in["res"].wait()
     flat = iota((1, WIDTH), 1)
     flat_face = face_at(flat, FACE)
@@ -272,28 +290,22 @@
     rr_row = row_of(0.5 * jnp.sum(res * res, axis=1, keepdims=True))
     wait_recv(nb_rf, 0)
     own_load = jnp.zeros((8, 128), F32)
-    curvature = jnp.zeros((CASES, 128), F32)
     nb_load = []
     for f in range(4):
         cut = slice(f * PAD, (f + 1) * PAD)
         nb_rf[f] = jnp.where(active_pad[:, cut], nb_rf[f], 0.0)
-        r_high, r_low = split(jnp.concatenate([own_rf[f], nb_rf[f]], axis=0))
+        r_high, r_low = split(jnp.concatenate([own_rf[f, :, :ROWS], nb_rf[f, :, :ROWS]], axis=0))
         y_high, y_low = split(ys[f])
         piece = mm(
-            jnp.concatenate([r_high, r_low, dir_high[:, cut], dir_low[:, cut]], axis=0),
-            jnp.concatenate([y_high, y_low], axis=1),
-            NN,
+            jnp.concatenate([r_high, r_low], axis=0), jnp.concatenate([y_high, y_low], axis=1), NN
         )
         piece = piece[:, :128] + piece[:, 128:]
-        curvature = curvature + piece[32 : 32 + CASES] + piece[32 + CASES :]
         piece = piece[:16] + piece[16:32]
         if not f & 1:
             piece = -piece
         own_load = own_load + piece[:8]
         nb_load.append(summed(piece[8:]))
     own_load = summed(own_load)
-    diagonal = (iota((CASES, 128), 1) & 63) == iota((CASES, 128), 0)
-    curv_row = summed(jnp.sum(jnp.where(diagonal, curvature, 0.0), axis=0, keepdims=True))
     own_load = jnp.where(row == 6, rr_row, jnp.where(row == 7, curv_row, own_load))
     for f in range(3):
         moved = pltpu.roll(nb_load[3], 6 - 2 * f, 0)
@@ -303,11 +315,11 @@
     for step in range(1, MATES):
         send(loads.at[place], loads.at[place], 2, mate(step))
     for f in range(4):
-        y = jnp.transpose(ys[f])
+        y = jnp.transpose(jnp.concatenate([ys[f], jnp.zeros((PAD - ROWS, 128), F32)], axis=0))
         y = (y[:CASES] + y[CASES:]) * mask_pad[:, f * PAD : (f + 1) * PAD]
         own_y[f] = y
         send(own_y.at[f], nb_y.at[f ^ 1], 3, across[f])
-    res = padded(res)
+    res = padded(res, PAD)
     for f in range(4):
         res_pad[f] = res[:, f * PAD : (f + 1) * PAD]
 
@@ -352,14 +364,15 @@
         )
         gram = gram + piece[:8] + piece[8:]
     grams[place] = gram
-    for step in range(1, MATES):
-        send(grams.at[place], grams.at[place], 4, mate(step))
 
     rows_in[pair] = rows_out[pair]
-    wait_recv(rows_in.at[0 : PAIRS - 1], 1)
+    wait_recv(rows_in.at[0 : PAIRS - 1, 0:MODES], 1)
     high, low = split(rows_in[...].reshape(PAIRS * 8, 128))
     piece = mm(jnp.concatenate([high, low], axis=0), pick, NN).astype(BF16)
     piece = jnp.concatenate([piece[: PAIRS * 8], piece[PAIRS * 8 :]], axis=1)
+
+    for step in range(1, MATES):
+        send(grams.at[place], grams.at[place], 4, mate(step))
 
     wait_recv(loads.at[0 : MATES - 1], 2)
     every = loads[...]
@@ -368,7 +381,7 @@
     part = summed(mm(piece, jnp.concatenate([line, line], axis=0), NN))
     part = part.reshape(PAIRS, 8, 128) + jnp.where(row >= MODES, total, 0.0)[None]
     parts[...] = jnp.where(left[None], part, pltpu.roll(part, 4, 1))[:, 0:4, :]
-    for step in range(1, PAIRS):
+    for step in PEERS:
         other, target = peer(step)
         send(parts.at[other], got.at[pair], 5, target)
     got[pair] = parts[pair]
@@ -426,7 +439,7 @@
     spare = (iota((MATES * 8, 128), 0) & 7) >= MODES
     norm = jnp.sum(jnp.where(spare, mates, mates * image), axis=0, keepdims=True)
     norms[pair] = norm
-    for step in range(1, PAIRS):
+    for step in PEERS:
         send(norms.at[pair], norms.at[pair], 7, peer(step)[1])
 
     spread = []
@@ -443,11 +456,13 @@
     next_copy = pltpu.make_async_copy(next_v, res_out, out_sem.at[0])
     next_copy.start()
     wait_recv(norms.at[0 : PAIRS - 1], 7)
-    ratio = column_of(jnp.sum(norms[...], axis=0) / rr_row)
-    coef_out[...] = jnp.where(iota((CASES, 128), 1) < 64, step_size, ratio)
+    ratio = jnp.sum(norms[...], axis=0) / rr_row
+    coef_v[...] = jnp.where(row == 0, step_row, ratio)
+    coef_copy = pltpu.make_async_copy(coef_v, coef_out, out_sem.at[1])
+    coef_copy.start()
 
     wait_send(own_rf, 0)
-    wait_send(rows_in.at[0 : PAIRS - 1], 1)
+    wait_send(rows_in.at[0 : PAIRS - 1, 0:MODES], 1)
     wait_send(loads.at[0 : MATES - 1], 2)
     wait_send(own_y, 3)
     wait_send(grams.at[0 : MATES - 1], 4)
@@ -455,6 +470,7 @@
     wait_send(amps.at[0:15], 6)
     wait_send(norms.at[0 : PAIRS - 1], 7)
     next_copy.wait()
+    coef_copy.wait()
 
 
 def update(
@@ -473,46 +489,41 @@
     dir_v,
     sem,
 ):
+    first = [
+        pltpu.make_async_copy(sizes_hbm, sizes_ref, sem.at[0]),
+        pltpu.make_async_copy(coef_hbm, coef_v, sem.at[1]),
+    ]
     ins = [
-        pltpu.make_async_copy(src, dst, sem.at[k])
-        for k, (src, dst) in enumerate(
-            (
-                (sizes_hbm, sizes_ref),
-                (dir_hbm, dir_v),
-                (lam_hbm, lam_v),
-                (coef_hbm, coef_v),
-                (res_hbm, res_v),
-            )
-        )
+        pltpu.make_async_copy(src, dst, sem.at[2 + k])
+        for k, (src, dst) in enumerate(((dir_hbm, dir_v), (lam_hbm, lam_v), (res_hbm, res_v)))
     ]
-    for copy in ins:
-        copy.start()
     outs = [
         pltpu.make_async_copy(src, dst, sem.at[5 + k])
         for k, (src, dst) in enumerate(((lam_v, lam_out), (res_v, res_out), (dir_v, dir_out)))
     ]
-    ins[0].wait()
+    for one in first + ins:
+        one.start()
+    first[0].wait()
     flat = iota((1, WIDTH), 1)
     face = face_at(flat, FACE)
     limit = jnp.zeros_like(face)
     for f in range(4):
         limit = jnp.where(face == f, sizes_ref[0, 0, f], limit)
     active = (flat - face * FACE) < limit
-    ins[1].wait()
+    first[1].wait()
+    step_size = column_of(coef_v[0:1, :])
+    ratio = column_of(coef_v[1:2, :])
+    for one in ins[0:2]:
+        one.wait()
     dirn = jnp.where(active, dir_v[...], 0.0)
-    ins[2].wait()
-    ins[3].wait()
-    coef = coef_v[...]
-    step_size = coef[:, 0:1]
-    ratio = coef[:, 64:65]
     lam_v[...] = jnp.where(active, lam_v[...], 0.0) + step_size * dirn
     outs[0].start()
-    ins[4].wait()
+    ins[2].wait()
     outs[1].start()
     dir_v[...] = res_v[...] + ratio * dirn
     outs[2].start()
-    for copy in outs:
-        copy.wait()
+    for one in outs:
+        one.wait()
 
 
 def on_device(
@@ -527,14 +538,14 @@
 ):
     field = jax.ShapeDtypeStruct((CASES, WIDTH), F32)
     hbm = pl.BlockSpec(memory_space=pltpu.HBM)
-    vmem = pl.BlockSpec(memory_space=pltpu.VMEM)
     res_next, coef = pl.pallas_call(
         kernel,
-        out_shape=(field, jax.ShapeDtypeStruct((CASES, 128), F32)),
+        out_shape=(field, jax.ShapeDtypeStruct((8, 128), F32)),
         in_specs=[hbm] * 7,
-        out_specs=[hbm, vmem],
+        out_specs=[hbm, hbm],
         scratch_shapes=[
             pltpu.VMEM((CASES, WIDTH), F32),
+            pltpu.VMEM((8, 128), F32),
             pltpu.VMEM((CASES, WIDTH), F32),
             pltpu.VMEM((CASES, WIDTH), F32),
             pltpu.VMEM((WIDTH, WIDTH), F32),
@@ -542,7 +553,7 @@
             pltpu.VMEM((MODES, COARSE), F32),
             pltpu.VMEM((1, 1, WIDTH), jnp.int32),
             pltpu.SMEM((1, 1, 4), jnp.int32),
-            pltpu.VMEM((WIDE, WIDTH), BF16),
+            pltpu.VMEM((4 * ROWS, WIDTH), BF16),
             pltpu.VMEM((WIDTH, 256), BF16),
             pltpu.VMEM((4, 8, PAD), F32),
             pltpu.VMEM((4, 8, PAD), F32),
@@ -558,7 +569,7 @@
             pltpu.VMEM((16, 4, 128), F32),
             pltpu.VMEM((PAIRS, 1, 128), F32),
             pltpu.SemaphoreType.DMA((7,)),
-            pltpu.SemaphoreType.DMA((1,)),
+            pltpu.SemaphoreType.DMA((2,)),
             pltpu.SemaphoreType.DMA((8,)),
             pltpu.SemaphoreType.DMA((8,)),
         ],
@@ -580,7 +591,7 @@
         in_specs=[hbm] * 5,
         out_specs=[hbm, hbm, hbm],
         scratch_shapes=[
-            pltpu.VMEM((CASES, 128), F32),
+            pltpu.VMEM((8, 128), F32),
             pltpu.SMEM((1, 1, 4), jnp.int32),
             pltpu.VMEM((CASES, WIDTH), F32),
             pltpu.VMEM((CASES, WIDTH), F32),

time: 39.6 us -> 38.9 us (0.982)
  Pallas kernels: 38.8 us -> 38.1 us
    pallas_call x1, Pallas kernels: 36.7 us -> 36 us  [on_device(): pl.pallas_call(kernel, out_shape=(field, jax.ShapeDtypeStruct((8, 128), F...]
where the time goes in v4:
time: 38.9 us; the launch traced here: 38.8 us
  Pallas kernels  38.1 us (98%)
  between operations  0.64 us (2%)
    pallas_call x1, Pallas kernels, on_device(): pl.pallas_call(kernel, out_shape=(field, jax.ShapeDtypeStruct((8, 128), F...  36 us
    pallas_call x1, Pallas kernels, on_device(): pl.pallas_call(update, out_shape=(field, field, field), in_specs=[hbm] *...  2.13 us

profile of v4, /device:TPU:1, one launch (start us, length us, event | category | flops | bytes accessed | tf_op | source)
XLA Modules:
  0.0 38.8 jit_solution(3422277433091822281)
XLA Ops:
  0.6 36.0 %shard_map.103 = (f32[64,1200]{1,0:T(8,128)}, f32[8,128]{1,0:T(8,128)}) custom-call(f32[64,1200]{1,0:T(8,128)} %bitcast.11, f32[64,1200]{1,0:T(8,128)} %bitcast.9, f32[1200,1200]{1,0:T(8,128)} %bitcast.8, f32[6,1,1200]{2,1,0:T(1,128)} %bitcast.13, f32[6,1536]{1,0:T(8,128)} %inv_hbm.1, s32[1,1,4]{2,1,0:T(1,128)} %sizes_hbm.3, s32[1,1,1200]{2,1,0:T(1,128)} %order_hbm.1), custom_call_target="tpu_custom_call" | custom-call | tf_op jit(solution)/shard_map/pallas_call | solution.py:541
  36.6 2.1 %shard_map.104 = (f32[64,1200]{1,0:T(8,128)}, f32[64,1200]{1,0:T(8,128)}, f32[64,1200]{1,0:T(8,128)}) custom-call(f32[64,1200]{1,0:T(8,128)} %bitcast.12, f32[64,1200]{1,0:T(8,128)} %bitcast.10, f32[64,1200]{1,0:T(8,128)} %get-tuple-element.8.res_hbm, f32[8,128]{1,0:T(8,128)} %get-tuple-element.9.coef_hbm, s32[1,1,4]{2,1,0:T(1,128)} %sizes_hbm.3), custom_call_target="tpu_custom_call" | custom-call | tf_op jit(solution)/shard_map/pallas_call | solution.py:588

commit v5 on v4

--- a/solution.py
+++ b/solution.py
@@ -125,8 +125,10 @@
     loads,
     parts,
     got,
+    got_next,
     grams,
     amps,
+    amp_before,
     norms,
     in_sem,
     out_sem,
@@ -171,14 +173,22 @@
         other = (pair // 8 + dx) % 4 * 8 + (pair + dz) % 8
         return other, (other * 2 + core, g)
 
-    beside = (pair + 2 * core - 1 + PAIRS) % PAIRS
+    has_next = (core == 1) & (pair < PAIRS - 1)
+    has_before = (core == 0) & (pair > 0)
 
     barrier = pltpu.get_barrier_semaphore()
     for step in PEERS:
         pl.semaphore_signal(barrier, inc=1, device_id=peer(step)[1], device_id_type=MESH)
-    for other in range(4):
-        for target in ((2 * pair + 63) % 64, other), ((2 * pair + 2) % 64, other):
-            pl.semaphore_signal(barrier, inc=1, device_id=target, device_id_type=MESH)
+    pl.semaphore_signal(
+        barrier, inc=1, device_id=((s + 2 * core + 63) % 64, g), device_id_type=MESH
+    )
+
+    @pl.when(core == 1)
+    def _():
+        for step in PEERS:
+            other = peer(step)[0]
+            pl.semaphore_signal(barrier, inc=1, device_id=(2 * other, g), device_id_type=MESH)
+
     for step in range(1, MATES):
         pl.semaphore_signal(barrier, inc=1, device_id=mate(step), device_id_type=MESH)
 
@@ -199,7 +209,7 @@
         pltpu.make_async_copy(ref, ref, send_sem.at[phase]).wait()
 
     def greeted():
-        pl.semaphore_wait(barrier, PAIRS - 1 + 8 + MATES - 1)
+        pl.semaphore_wait(barrier, (PAIRS - 1) * (2 - core) + 1 + MATES - 1)
         for f in range(4):
             send(own_rf.at[f], nb_rf.at[f ^ 1], 0, across[f])
         for step in PEERS:
@@ -338,15 +348,15 @@
 
     slots_of = (
         place,
-        core * g + (1 - core) * (8 + g),
-        core * (12 + g) + (1 - core) * (4 + g),
+        core * g + (1 - core) * MATES,
+        core * MATES + (1 - core) * (4 + g),
         core * 4 + (g + 3) % 4,
         core * 4 + (g + 1) % 4,
     )
     lane = iota((32, 128), 1)
     line = iota((32, 128), 0)
-    mode = 4 * (lane >> 6) + (lane & 3)
-    slot = (lane >> 2) & 15
+    mode = 4 * (lane >> 5) + (lane & 3)
+    slot = (lane >> 2) & 7
     gram = jnp.zeros((8, 128), F32)
     for f in range(4):
         r_high, r_low = split(own_rf[f])
@@ -354,7 +364,10 @@
         piece = mm(
             jnp.concatenate([r_high, r_low], axis=0), jnp.concatenate([n_high, n_low], axis=0), NT
         )
-        piece_high, piece_low = split(piece[:8] + piece[8:])
+        piece = piece[:8] + piece[8:]
+        if f == 1:
+            edge = piece[:, 8:16]
+        piece_high, piece_low = split(piece)
         wanted = jnp.where((line & 8) == 0, slots_of[0], slots_of[1 + f])
         hot = ((line & 7) == mode) & (mode < MODES) & (slot == wanted)
         piece = mm(
@@ -381,9 +394,20 @@
     part = summed(mm(piece, jnp.concatenate([line, line], axis=0), NN))
     part = part.reshape(PAIRS, 8, 128) + jnp.where(row >= MODES, total, 0.0)[None]
     parts[...] = jnp.where(left[None], part, pltpu.roll(part, 4, 1))[:, 0:4, :]
-    for step in PEERS:
-        other, target = peer(step)
-        send(parts.at[other], got.at[pair], 5, target)
+    @pl.when(core == 0)
+    def _():
+        for step in PEERS:
+            other, target = peer(step)
+            send(parts.at[other], got_next.at[pair], 8, ((2 * other + 63) % 64, g))
+            send(parts.at[other], got.at[pair], 5, target)
+        send(parts.at[pair], got_next.at[pair], 8, ((2 * pair + 63) % 64, g))
+
+    @pl.when(core == 1)
+    def _():
+        for step in PEERS:
+            other, target = peer(step)
+            send(parts.at[other], got.at[pair], 5, target)
+
     got[pair] = parts[pair]
 
     wait_recv(nb_y, 3)
@@ -407,10 +431,10 @@
     trace_res = summed(trace_res)
     trace_image = summed(trace_image)
     wait_recv(grams.at[0 : MATES - 1], 4)
-    high, low = split(grams[...].reshape(MATES * 8, 128))
-    gram = jnp.concatenate([high, low], axis=1)
+    gram = lanes_split(summed(grams[...].reshape(MATES * 8, 128)))
 
     wait_recv(got.at[0 : PAIRS - 1], 5)
+    pl.when(core == 1)(lambda: wait_recv(got_next, 8))
     amp = doubled(unpacked(jnp.sum(got[...], axis=0)))
     rr_row = amp[6:7, :]
     step_row = rr_row / amp[7:8, :]
@@ -423,28 +447,43 @@
             square = square + u[:, k : k + 128] * u[:, k : k + 128]
     u_row = row_of(0.5 * jnp.sum(square, axis=1, keepdims=True))
     scaled = jnp.where(row < MODES, step_row * amp, 0.0)
-    cross = jnp.sum(scaled * (trace_res - step_row * trace_image), axis=0, keepdims=True)
+    after = doubled(unpacked(jnp.sum(got_next[...], axis=0)))
+    after = jnp.where((row < MODES) & has_next, step_row * after, 0.0)
+    cross = trace_res - step_row * trace_image
+    for k in range(MODES):
+        cross = cross + edge[:, k : k + 1] * after[k : k + 1, :]
+    cross = jnp.sum(scaled * cross, axis=0, keepdims=True)
     own = jnp.where(row == 6, doubled(u_row + 2.0 * cross), scaled)
     amps[place] = packed(own)
-    slot = 12 - 4 * core + g
-    for other in range(8):
-        send(amps.at[place], amps.at[slot], 6, (2 * beside + other // 4, other % 4))
     for step in range(1, MATES):
         send(amps.at[place], amps.at[place], 6, mate(step))
-    wait_recv(amps.at[0:15], 6)
+
+    @pl.when(has_next)
+    def _():
+        send(amps.at[place], amp_before, 9, (2 * pair + 2, g))
+
+    wait_recv(amps.at[0 : MATES - 1], 6)
     every = amps[...]
-    line = both_sides(every.reshape(64, 128))
+    line = both_sides(every.reshape(MATES * 4, 128))
     image = summed(mm(gram, jnp.concatenate([line, line], axis=0), NN))
-    mates = unpacked(every[0:MATES]).reshape(MATES * 8, 128)
+    mates = unpacked(every).reshape(MATES * 8, 128)
     spare = (iota((MATES * 8, 128), 0) & 7) >= MODES
     norm = jnp.sum(jnp.where(spare, mates, mates * image), axis=0, keepdims=True)
     norms[pair] = norm
     for step in PEERS:
         send(norms.at[pair], norms.at[pair], 7, peer(step)[1])
 
+    pl.when(has_before)(lambda: wait_recv(amp_before, 9))
     spread = []
     for f in range(4):
-        a_high, a_low = split(jnp.concatenate([own, unpacked(amps[slots_of[1 + f]])], axis=0))
+        if f == 0:
+            there = unpacked(jnp.where(core == 1, amps[g], amp_before[...]))
+            there = jnp.where(has_before | (core == 1), there, 0.0)
+        elif f == 1:
+            there = jnp.where(core == 1, after, unpacked(amps[4 + g]))
+        else:
+            there = unpacked(amps[slots_of[1 + f]])
+        a_high, a_low = split(jnp.concatenate([own, there], axis=0))
         r_high, r_low = split(jnp.concatenate([own_rf[f], nb_rf[f]], axis=0))
         back = mm(
             jnp.concatenate([a_high, a_low, a_high, a_low], axis=0),
@@ -467,7 +506,9 @@
     wait_send(own_y, 3)
     wait_send(grams.at[0 : MATES - 1], 4)
     wait_send(parts.at[0 : PAIRS - 1], 5)
-    wait_send(amps.at[0:15], 6)
+    wait_send(amps.at[0 : MATES - 1], 6)
+    pl.when(has_next)(lambda: wait_send(amp_before, 9))
+    pl.when(core == 0)(lambda: wait_send(got_next, 8))
     wait_send(norms.at[0 : PAIRS - 1], 7)
     next_copy.wait()
     coef_copy.wait()
@@ -565,13 +606,15 @@
             pltpu.VMEM((MATES, 16, 128), F32),
             pltpu.VMEM((PAIRS, 4, 128), F32),
             pltpu.VMEM((PAIRS, 4, 128), F32),
+            pltpu.VMEM((PAIRS, 4, 128), F32),
             pltpu.VMEM((MATES, 8, 128), F32),
-            pltpu.VMEM((16, 4, 128), F32),
+            pltpu.VMEM((MATES, 4, 128), F32),
+            pltpu.VMEM((4, 128), F32),
             pltpu.VMEM((PAIRS, 1, 128), F32),
             pltpu.SemaphoreType.DMA((7,)),
             pltpu.SemaphoreType.DMA((2,)),
-            pltpu.SemaphoreType.DMA((8,)),
-            pltpu.SemaphoreType.DMA((8,)),
+            pltpu.SemaphoreType.DMA((10,)),
+            pltpu.SemaphoreType.DMA((10,)),
         ],
         compiler_params=pltpu.CompilerParams(
             collective_id=0, has_side_effects=True, vmem_limit_bytes=62 * 1024 * 1024

time: 38.9 us -> 38.6 us (level)
  no operation moved by 1% of the time
where the time goes in v5:
time: 38.6 us; the launch traced here: 38.5 us
  Pallas kernels  37.8 us (98%)
  between operations  0.64 us (2%)
    pallas_call x1, Pallas kernels, on_device(): pl.pallas_call(kernel, out_shape=(field, jax.ShapeDtypeStruct((8, 128), F...  35.7 us
    pallas_call x1, Pallas kernels, on_device(): pl.pallas_call(update, out_shape=(field, field, field), in_specs=[hbm] *...  2.13 us

profile of v5, /device:TPU:1, one launch (start us, length us, event | category | flops | bytes accessed | tf_op | source)
XLA Modules:
  0.0 38.5 jit_solution(7884056367238923781)
XLA Ops:
  0.6 35.7 %shard_map.103 = (f32[64,1200]{1,0:T(8,128)}, f32[8,128]{1,0:T(8,128)}) custom-call(f32[64,1200]{1,0:T(8,128)} %bitcast.11, f32[64,1200]{1,0:T(8,128)} %bitcast.9, f32[1200,1200]{1,0:T(8,128)} %bitcast.8, f32[6,1,1200]{2,1,0:T(1,128)} %bitcast.13, f32[6,1536]{1,0:T(8,128)} %inv_hbm.1, s32[1,1,4]{2,1,0:T(1,128)} %sizes_hbm.3, s32[1,1,1200]{2,1,0:T(1,128)} %order_hbm.1), custom_call_target="tpu_custom_call" | custom-call | tf_op jit(solution)/shard_map/pallas_call | solution.py:582
  36.4 2.1 %shard_map.104 = (f32[64,1200]{1,0:T(8,128)}, f32[64,1200]{1,0:T(8,128)}, f32[64,1200]{1,0:T(8,128)}) custom-call(f32[64,1200]{1,0:T(8,128)} %bitcast.12, f32[64,1200]{1,0:T(8,128)} %bitcast.10, f32[64,1200]{1,0:T(8,128)} %get-tuple-element.8.res_hbm, f32[8,128]{1,0:T(8,128)} %get-tuple-element.9.coef_hbm, s32[1,1,4]{2,1,0:T(1,128)} %sizes_hbm.3), custom_call_target="tpu_custom_call" | custom-call | tf_op jit(solution)/shard_map/pallas_call | solution.py:631

commit v6 on v5

--- a/solution.py
+++ b/solution.py
@@ -102,8 +102,7 @@
     inv_hbm,
     sizes_hbm,
     order_hbm,
-    res_out,
-    coef_out,
+    next_out,
     next_v,
     coef_v,
     res_v,
@@ -129,6 +128,7 @@
     grams,
     amps,
     amp_before,
+    scalars,
     norms,
     in_sem,
     out_sem,
@@ -434,10 +434,18 @@
     gram = lanes_split(summed(grams[...].reshape(MATES * 8, 128)))
 
     wait_recv(got.at[0 : PAIRS - 1], 5)
-    pl.when(core == 1)(lambda: wait_recv(got_next, 8))
     amp = doubled(unpacked(jnp.sum(got[...], axis=0)))
     rr_row = amp[6:7, :]
     step_row = rr_row / amp[7:8, :]
+    scaled = jnp.where(row < MODES, step_row * amp, 0.0)
+    amps[place] = packed(scaled)
+    for step in range(1, MATES):
+        send(amps.at[place], amps.at[place], 6, mate(step))
+
+    @pl.when(has_next)
+    def _():
+        send(amps.at[place], amp_before, 9, (2 * pair + 2, g))
+
     step_size = column_of(step_row)
     square = jnp.zeros((CASES, 128), F32)
     for f in range(4):
@@ -446,30 +454,25 @@
         for k in range(0, PAD, 128):
             square = square + u[:, k : k + 128] * u[:, k : k + 128]
     u_row = row_of(0.5 * jnp.sum(square, axis=1, keepdims=True))
-    scaled = jnp.where(row < MODES, step_row * amp, 0.0)
+    cross = trace_res - step_row * trace_image
+    pl.when(core == 1)(lambda: wait_recv(got_next, 8))
     after = doubled(unpacked(jnp.sum(got_next[...], axis=0)))
     after = jnp.where((row < MODES) & has_next, step_row * after, 0.0)
-    cross = trace_res - step_row * trace_image
     for k in range(MODES):
         cross = cross + edge[:, k : k + 1] * after[k : k + 1, :]
     cross = jnp.sum(scaled * cross, axis=0, keepdims=True)
-    own = jnp.where(row == 6, doubled(u_row + 2.0 * cross), scaled)
-    amps[place] = packed(own)
+    scalars[place] = doubled(u_row + 2.0 * cross)
     for step in range(1, MATES):
-        send(amps.at[place], amps.at[place], 6, mate(step))
-
-    @pl.when(has_next)
-    def _():
-        send(amps.at[place], amp_before, 9, (2 * pair + 2, g))
+        send(scalars.at[place], scalars.at[place], 10, mate(step))
 
     wait_recv(amps.at[0 : MATES - 1], 6)
     every = amps[...]
     line = both_sides(every.reshape(MATES * 4, 128))
     image = summed(mm(gram, jnp.concatenate([line, line], axis=0), NN))
     mates = unpacked(every).reshape(MATES * 8, 128)
-    spare = (iota((MATES * 8, 128), 0) & 7) >= MODES
-    norm = jnp.sum(jnp.where(spare, mates, mates * image), axis=0, keepdims=True)
-    norms[pair] = norm
+    norm = jnp.sum(mates * image, axis=0, keepdims=True)
+    wait_recv(scalars.at[0 : MATES - 1], 10)
+    norms[pair] = norm + jnp.sum(scalars[...], axis=0)
     for step in PEERS:
         send(norms.at[pair], norms.at[pair], 7, peer(step)[1])
 
@@ -483,7 +486,7 @@
             there = jnp.where(core == 1, after, unpacked(amps[4 + g]))
         else:
             there = unpacked(amps[slots_of[1 + f]])
-        a_high, a_low = split(jnp.concatenate([own, there], axis=0))
+        a_high, a_low = split(jnp.concatenate([scaled, there], axis=0))
         r_high, r_low = split(jnp.concatenate([own_rf[f], nb_rf[f]], axis=0))
         back = mm(
             jnp.concatenate([a_high, a_low, a_high, a_low], axis=0),
@@ -492,12 +495,12 @@
         )
         spread.append((res_pad[f] + back[:CASES])[:, :FACE])
     next_v[...] = jnp.concatenate(spread, axis=1)
-    next_copy = pltpu.make_async_copy(next_v, res_out, out_sem.at[0])
+    next_copy = pltpu.make_async_copy(next_v, next_out.at[0:CASES], out_sem.at[0])
     next_copy.start()
     wait_recv(norms.at[0 : PAIRS - 1], 7)
     ratio = jnp.sum(norms[...], axis=0) / rr_row
     coef_v[...] = jnp.where(row == 0, step_row, ratio)
-    coef_copy = pltpu.make_async_copy(coef_v, coef_out, out_sem.at[1])
+    coef_copy = pltpu.make_async_copy(coef_v, next_out.at[CASES:, 0:128], out_sem.at[1])
     coef_copy.start()
 
     wait_send(own_rf, 0)
@@ -507,6 +510,7 @@
     wait_send(grams.at[0 : MATES - 1], 4)
     wait_send(parts.at[0 : PAIRS - 1], 5)
     wait_send(amps.at[0 : MATES - 1], 6)
+    wait_send(scalars.at[0 : MATES - 1], 10)
     pl.when(has_next)(lambda: wait_send(amp_before, 9))
     pl.when(core == 0)(lambda: wait_send(got_next, 8))
     wait_send(norms.at[0 : PAIRS - 1], 7)
@@ -515,10 +519,9 @@
 
 
 def update(
-    lam_hbm,
-    dir_hbm,
+    lam_ref,
+    dir_ref,
     res_hbm,
-    coef_hbm,
     sizes_hbm,
     lam_out,
     res_out,
@@ -530,34 +533,30 @@
     dir_v,
     sem,
 ):
-    first = [
-        pltpu.make_async_copy(sizes_hbm, sizes_ref, sem.at[0]),
-        pltpu.make_async_copy(coef_hbm, coef_v, sem.at[1]),
-    ]
     ins = [
-        pltpu.make_async_copy(src, dst, sem.at[2 + k])
-        for k, (src, dst) in enumerate(((dir_hbm, dir_v), (lam_hbm, lam_v), (res_hbm, res_v)))
+        pltpu.make_async_copy(src, dst, sem.at[k])
+        for k, (src, dst) in enumerate(
+            ((sizes_hbm, sizes_ref), (res_hbm.at[CASES:, 0:128], coef_v), (res_hbm.at[0:CASES], res_v))
+        )
     ]
     outs = [
-        pltpu.make_async_copy(src, dst, sem.at[5 + k])
+        pltpu.make_async_copy(src, dst, sem.at[3 + k])
         for k, (src, dst) in enumerate(((lam_v, lam_out), (res_v, res_out), (dir_v, dir_out)))
     ]
-    for one in first + ins:
+    for one in ins:
         one.start()
-    first[0].wait()
+    ins[0].wait()
     flat = iota((1, WIDTH), 1)
     face = face_at(flat, FACE)
     limit = jnp.zeros_like(face)
     for f in range(4):
         limit = jnp.where(face == f, sizes_ref[0, 0, f], limit)
     active = (flat - face * FACE) < limit
-    first[1].wait()
+    dirn = jnp.where(active, dir_ref[...], 0.0)
+    ins[1].wait()
     step_size = column_of(coef_v[0:1, :])
     ratio = column_of(coef_v[1:2, :])
-    for one in ins[0:2]:
-        one.wait()
-    dirn = jnp.where(active, dir_v[...], 0.0)
-    lam_v[...] = jnp.where(active, lam_v[...], 0.0) + step_size * dirn
+    lam_v[...] = jnp.where(active, lam_ref[...], 0.0) + step_size * dirn
     outs[0].start()
     ins[2].wait()
     outs[1].start()
@@ -579,11 +578,12 @@
 ):
     field = jax.ShapeDtypeStruct((CASES, WIDTH), F32)
     hbm = pl.BlockSpec(memory_space=pltpu.HBM)
-    res_next, coef = pl.pallas_call(
+    vmem = pl.BlockSpec(memory_space=pltpu.VMEM)
+    res_next = pl.pallas_call(
         kernel,
-        out_shape=(field, jax.ShapeDtypeStruct((8, 128), F32)),
+        out_shape=jax.ShapeDtypeStruct((CASES + 8, WIDTH), F32),
         in_specs=[hbm] * 7,
-        out_specs=[hbm, hbm],
+        out_specs=hbm,
         scratch_shapes=[
             pltpu.VMEM((CASES, WIDTH), F32),
             pltpu.VMEM((8, 128), F32),
@@ -610,11 +610,12 @@
             pltpu.VMEM((MATES, 8, 128), F32),
             pltpu.VMEM((MATES, 4, 128), F32),
             pltpu.VMEM((4, 128), F32),
+            pltpu.VMEM((MATES, 1, 128), F32),
             pltpu.VMEM((PAIRS, 1, 128), F32),
             pltpu.SemaphoreType.DMA((7,)),
             pltpu.SemaphoreType.DMA((2,)),
-            pltpu.SemaphoreType.DMA((10,)),
-            pltpu.SemaphoreType.DMA((10,)),
+            pltpu.SemaphoreType.DMA((11,)),
+            pltpu.SemaphoreType.DMA((11,)),
         ],
         compiler_params=pltpu.CompilerParams(
             collective_id=0, has_side_effects=True, vmem_limit_bytes=62 * 1024 * 1024
@@ -631,7 +632,7 @@
     outs = pl.pallas_call(
         update,
         out_shape=(field, field, field),
-        in_specs=[hbm] * 5,
+        in_specs=[vmem, vmem, hbm, hbm],
         out_specs=[hbm, hbm, hbm],
         scratch_shapes=[
             pltpu.VMEM((8, 128), F32),
@@ -639,14 +640,13 @@
             pltpu.VMEM((CASES, WIDTH), F32),
             pltpu.VMEM((CASES, WIDTH), F32),
             pltpu.VMEM((CASES, WIDTH), F32),
-            pltpu.SemaphoreType.DMA((8,)),
+            pltpu.SemaphoreType.DMA((6,)),
         ],
-        compiler_params=pltpu.CompilerParams(vmem_limit_bytes=62 * 1024 * 1024),
+        compiler_params=pltpu.CompilerParams(vmem_limit_bytes=55600000),
     )(
         multipliers.reshape(CASES, WIDTH),
         direction.reshape(CASES, WIDTH),
         res_next,
-        coef,
         face_sizes,
     )
     return tuple(x[None, None] for x in outs)

time: 38.6 us -> 38.1 us (0.987)
  Pallas kernels: 37.8 us -> 37.3 us
    pallas_call x2, Pallas kernels: 37.8 us -> 37.3 us  [the longest x1 35.4 us: on_device(): pl.pallas_call(kernel, out_shape=jax.ShapeDtypeStruct((CASES + 8, WIDTH),...]
where the time goes in v6:
time: 38.1 us; the launch traced here: 38 us
  Pallas kernels  37.3 us (98%)
  between operations  0.69 us (2%)
    pallas_call x1, Pallas kernels, on_device(): pl.pallas_call(kernel, out_shape=jax.ShapeDtypeStruct((CASES + 8, WIDTH),...  35.4 us
    pallas_call x1, Pallas kernels, on_device(): pl.pallas_call(update, out_shape=(field, field, field), in_specs=[vmem, v...  1.86 us

profile of v6, /device:TPU:1, one launch (start us, length us, event | category | flops | bytes accessed | tf_op | source)
XLA Modules:
  0.0 38.0 jit_solution(13173994854168312035)
XLA Ops:
  0.6 0.0 copy-start.2
  0.6 0.0 copy-start
  0.7 0.0 copy-start.1
  0.7 35.4 %shard_map.103.res_hbm = f32[72,1200]{1,0:T(8,128)} custom-call(f32[64,1200]{1,0:T(8,128)} %bitcast.12, f32[64,1200]{1,0:T(8,128)} %bitcast.8, f32[1200,1200]{1,0:T(8,128)} %bitcast.11, f32[6,1,1200]{2,1,0:T(1,128)} %bitcast.13, f32[6,1536]{1,0:T(8,128)} %inv_hbm.1, s32[1,1,4]{2,1,0:T(1,128)} %sizes_hbm.3, s32[1,1,1200]{2,1,0:T(1,128)} %order_hbm.1), custom_call_target="tpu_custom_call" | custom-call | tf_op jit(solution)/shard_map/pallas_call | solution.py:582
  36.1 0.0 copy-done.2
  36.1 0.0 copy-done
  36.1 0.0 copy-done.1
  36.1 1.9 %shard_map.104 = (f32[64,1200]{1,0:T(8,128)}, f32[64,1200]{1,0:T(8,128)}, f32[64,1200]{1,0:T(8,128)}) custom-call(f32[64,1200]{1,0:T(8,128)S(1)} %bitcast.10, f32[64,1200]{1,0:T(8,128)S(1)} %bitcast.9, f32[72,1200]{1,0:T(8,128)} %shard_map.103.res_hbm, s32[1,1,4]{2,1,0:T(1,128)S(1)} %copy-done.2), custom_call_target="tpu_custom_call" | custom-call | tf_op jit(solution)/shard_map/pallas_call | solution.py:632
Async XLA Ops:
  0.6 35.5 %copy-start.2 = (s32[1,1,4]{2,1,0:T(1,128)S(1)}, s32[1,1,4]{2,1,0:T(1,128)}, u32[]{:S(2)}) copy-start(s32[1,1,4]{2,1,0:T(1,128)} %sizes_hbm.3) | copy-start | bytes 52
  0.6 35.5 %copy-start = (f32[1,1,64,1200]{3,2,1,0:T(8,128)S(1)}, f32[1,1,64,1200]{3,2,1,0:T(8,128)}, u32[]{:S(2)}) copy-start(f32[1,1,64,1200]{3,2,1,0:T(8,128)} %param.10) | copy-start | bytes 921604
  0.7 35.5 %copy-start.1 = (f32[1,1,64,1200]{3,2,1,0:T(8,128)S(1)}, f32[1,1,64,1200]{3,2,1,0:T(8,128)}, u32[]{:S(2)}) copy-start(f32[1,1,64,1200]{3,2,1,0:T(8,128)} %param.8) | copy-start | bytes 921604

commit v7 on v6

--- a/solution.py
+++ b/solution.py
@@ -183,12 +183,6 @@
         barrier, inc=1, device_id=((s + 2 * core + 63) % 64, g), device_id_type=MESH
     )
 
-    @pl.when(core == 1)
-    def _():
-        for step in PEERS:
-            other = peer(step)[0]
-            pl.semaphore_signal(barrier, inc=1, device_id=(2 * other, g), device_id_type=MESH)
-
     for step in range(1, MATES):
         pl.semaphore_signal(barrier, inc=1, device_id=mate(step), device_id_type=MESH)
 
@@ -209,7 +203,7 @@
         pltpu.make_async_copy(ref, ref, send_sem.at[phase]).wait()
 
     def greeted():
-        pl.semaphore_wait(barrier, (PAIRS - 1) * (2 - core) + 1 + MATES - 1)
+        pl.semaphore_wait(barrier, PAIRS - 1 + 1 + MATES - 1)
         for f in range(4):
             send(own_rf.at[f], nb_rf.at[f ^ 1], 0, across[f])
         for step in PEERS:

time: 38.1 us -> 38.1 us (level)
  no operation moved by 1% of the time
where the time goes in v7:
time: 38.1 us; the launch traced here: 38 us
  Pallas kernels  37.3 us (98%)
  between operations  0.69 us (2%)
    pallas_call x1, Pallas kernels, on_device(): pl.pallas_call(kernel, out_shape=jax.ShapeDtypeStruct((CASES + 8, WIDTH),...  35.4 us
    pallas_call x1, Pallas kernels, on_device(): pl.pallas_call(update, out_shape=(field, field, field), in_specs=[vmem, v...  1.86 us

profile of v7, /device:TPU:1, one launch (start us, length us, event | category | flops | bytes accessed | tf_op | source)
XLA Modules:
  0.0 38.0 jit_solution(10220108166747779544)
XLA Ops:
  0.6 0.0 copy-start.2
  0.6 0.0 copy-start
  0.7 0.0 copy-start.1
  0.7 35.4 %shard_map.103.res_hbm = f32[72,1200]{1,0:T(8,128)} custom-call(f32[64,1200]{1,0:T(8,128)} %bitcast.12, f32[64,1200]{1,0:T(8,128)} %bitcast.8, f32[1200,1200]{1,0:T(8,128)} %bitcast.11, f32[6,1,1200]{2,1,0:T(1,128)} %bitcast.13, f32[6,1536]{1,0:T(8,128)} %inv_hbm.1, s32[1,1,4]{2,1,0:T(1,128)} %sizes_hbm.3, s32[1,1,1200]{2,1,0:T(1,128)} %order_hbm.1), custom_call_target="tpu_custom_call" | custom-call | tf_op jit(solution)/shard_map/pallas_call | solution.py:576
  36.1 0.0 copy-done.2
  36.1 0.0 copy-done
  36.1 0.0 copy-done.1
  36.1 1.9 %shard_map.104 = (f32[64,1200]{1,0:T(8,128)}, f32[64,1200]{1,0:T(8,128)}, f32[64,1200]{1,0:T(8,128)}) custom-call(f32[64,1200]{1,0:T(8,128)S(1)} %bitcast.10, f32[64,1200]{1,0:T(8,128)S(1)} %bitcast.9, f32[72,1200]{1,0:T(8,128)} %shard_map.103.res_hbm, s32[1,1,4]{2,1,0:T(1,128)S(1)} %copy-done.2), custom_call_target="tpu_custom_call" | custom-call | tf_op jit(solution)/shard_map/pallas_call | solution.py:626
Async XLA Ops:
  0.6 35.5 %copy-start.2 = (s32[1,1,4]{2,1,0:T(1,128)S(1)}, s32[1,1,4]{2,1,0:T(1,128)}, u32[]{:S(2)}) copy-start(s32[1,1,4]{2,1,0:T(1,128)} %sizes_hbm.3) | copy-start | bytes 52
  0.6 35.5 %copy-start = (f32[1,1,64,1200]{3,2,1,0:T(8,128)S(1)}, f32[1,1,64,1200]{3,2,1,0:T(8,128)}, u32[]{:S(2)}) copy-start(f32[1,1,64,1200]{3,2,1,0:T(8,128)} %param.10) | copy-start | bytes 921604
  0.7 35.5 %copy-start.1 = (f32[1,1,64,1200]{3,2,1,0:T(8,128)S(1)}, f32[1,1,64,1200]{3,2,1,0:T(8,128)}, u32[]{:S(2)}) copy-start(f32[1,1,64,1200]{3,2,1,0:T(8,128)} %param.8) | copy-start | bytes 921604
